TPU v7x, 256 devices: a whole 4x4x8 slice. The times are simulated.
256 devices in a mesh: dom: 32 (over z, x), tile: 8 (over y, core).
Axes of the slice: x: 4, y: 4, z: 8, core: 2. Of those that a mesh axis runs over, the one named last changes fastest.
Arguments:
- features: bfloat16 [65536, 256], P('dom', 'tile'), may hold values from -6 to 6
- w_self: bfloat16 [256, 256], P('tile'), may hold values from -0.375 to 0.375
- w_neigh: bfloat16 [256, 256], P('tile'), may hold values from -0.375 to 0.375
- bias: float32 [256], replicated, may hold values from -3 to 3
- cotangent: bfloat16 [65536, 256], P('dom'), may hold values from -6 to 6
- hub_list: int32 [32, 16], P('dom'), may hold values from 0 to 2047, as said below
- send_list: int32 [32, 32, 512], P('dom'), may hold values from 0 to 2047
- send_count: int32 [32, 32], P('dom'), may hold values from 170 to 512, as said below
- tile_dst: int32 [32, 296], P('dom'), may hold values from 0 to 15
- tile_src: int32 [32, 296], P('dom'), may hold values from 0 to 147, as said below
- tile_count: int32 [32], P('dom'), may hold values from 148 to 296, as said below
- tile_mask: bfloat16 [32, 296, 128, 128], P('dom'), may hold values from 0 to 1, as said below
Outputs:
- hidden_out: bfloat16 [65536, 256], P('dom', 'tile')
- grad_features: float32 [65536, 256], P('dom', 'tile')
- grad_self: float32 [256, 256], P('tile')
- grad_neigh: float32 [256, 256], P('tile')
- grad_bias: float32 [256], replicated
Inputs may be any that keep to these rules, and one draw needn't show every extreme that they name: `hub_list`: the 16 entries of a row are distinct. `send_list`: slots s >= send_count[p, q] are not part of the list. `send_count`: some partition receives 512 rows from every partition. `tile_dst`: tiles at slots tile_count[q] and later are not part of the adjacency. `tile_src`: the first 148 tiles of each partition name every source block once. `tile_count`: some partition has 296 live tiles. `tile_mask`: entries are 0 or 1.
All inputs are finite; a program needn't handle non-finite values.
Results may differ from a plain program's by a relative error of at most 0.0029.
Values may be sent and summed in bfloat16 or wider, within the bound.
A program may use at most 128 MiB of HBM per device.

v0:
```python
import math

import jax
import jax.numpy as jnp
from jax import lax
from jax.sharding import PartitionSpec as P

BLK = 128
HUB_DEV = 16


def select_rows(indices, rows):
    table = (indices[:, None] == jnp.arange(rows.shape[0], dtype=jnp.int32)[None, :]).astype(
        rows.dtype
    )
    return jnp.dot(table, rows, preferred_element_type=jnp.float32).astype(rows.dtype)


def add_rows(total, indices, values):
    table = (jnp.arange(total.shape[0], dtype=jnp.int32)[:, None] == indices[None, :]).astype(
        jnp.float32
    )
    return total + jnp.dot(
        table, values, precision=lax.Precision.HIGHEST, preferred_element_type=jnp.float32
    )


def on_device(
    features,
    w_self,
    w_neigh,
    bias,
    cotangent,
    hub_list,
    send_list,
    send_count,
    tile_dst,
    tile_src,
    tile_count,
    tile_mask,
):
    domains = lax.axis_size("dom")
    tiles = lax.axis_size("tile")
    rows_here = features.shape[0]
    width = features.shape[1]
    dst_blocks = rows_here // BLK
    hubs_total = domains * HUB_DEV
    send_rows = send_list.shape[2]
    src_blocks = (rows_here + hubs_total + domains * send_rows) // BLK
    capacity = tile_mask.shape[1]
    group = min(8, domains)
    own_hubs = select_rows(hub_list[0], features)
    live_send = jnp.arange(send_rows, dtype=jnp.int32)[None, :] < send_count[0][:, None]
    grouped_lists = send_list[0].reshape(domains // group, group * send_rows)
    picked_rows = lax.map(lambda indices: select_rows(indices, features), grouped_lists)
    picked_rows = picked_rows.reshape(domains, send_rows, width)
    outgoing = jnp.where(live_send[:, :, None], picked_rows, jnp.zeros((), jnp.bfloat16))
    hub_rows = lax.all_gather(own_hubs, "dom", axis=0, tiled=True)
    incoming = lax.all_to_all(outgoing, "dom", split_axis=0, concat_axis=0, tiled=True)
    source = jnp.concatenate([features, hub_rows, incoming.reshape(-1, width)], axis=0).reshape(
        src_blocks, BLK, width
    )
    masks = tile_mask[0]
    dst_ids = tile_dst[0]
    src_ids = tile_src[0]
    live = jnp.arange(capacity, dtype=jnp.int32) < tile_count[0]
    src_match = src_ids[:, None] == jnp.arange(src_blocks, dtype=jnp.int32)[None, :]
    dst_match = dst_ids[:, None] == jnp.arange(dst_blocks, dtype=jnp.int32)[None, :]
    src_pick = src_match.astype(jnp.bfloat16)
    dst_pick = dst_match.astype(jnp.bfloat16)
    src_sum = (src_match & live[:, None]).astype(jnp.float32)
    dst_sum = (dst_match & live[:, None]).astype(jnp.float32)
    picked = jnp.einsum("tb,bjf->tjf", src_pick, source, preferred_element_type=jnp.float32).astype(
        jnp.bfloat16
    )
    products = jnp.einsum("tij,tjf->tif", masks, picked, preferred_element_type=jnp.float32)
    acc = jnp.einsum(
        "td,tif->dif",
        dst_sum,
        products,
        precision=lax.Precision.HIGHEST,
        preferred_element_type=jnp.float32,
    ).reshape(rows_here, width)
    row_sums = jnp.sum(masks, axis=2, dtype=jnp.float32)
    degree = jnp.einsum(
        "td,ti->di",
        dst_sum,
        row_sums,
        precision=lax.Precision.HIGHEST,
        preferred_element_type=jnp.float32,
    ).reshape(rows_here)
    floor = jnp.maximum(degree, 1.0)[:, None]
    agg = (acc / floor).astype(jnp.bfloat16)
    hid_width = w_self.shape[1] // tiles
    column_start = lax.axis_index("tile") * hid_width
    bias_here = lax.dynamic_slice_in_dim(bias, column_start, hid_width)
    partial_out = jnp.dot(features, w_self, preferred_element_type=jnp.float32) + jnp.dot(
        agg, w_neigh, preferred_element_type=jnp.float32
    )
    mixed = lax.psum_scatter(partial_out, "tile", scatter_dimension=1, tiled=True)
    hidden_out = (mixed + bias_here[None, :]).astype(jnp.bfloat16)
    scale = 1.0 / math.sqrt(domains * rows_here)
    contract_rows = (((0,), (0,)), ((), ()))
    self_term = lax.dot_general(
        features, cotangent, contract_rows, preferred_element_type=jnp.float32
    )
    neigh_term = lax.dot_general(agg, cotangent, contract_rows, preferred_element_type=jnp.float32)
    bias_term = jnp.sum(cotangent, axis=0, dtype=jnp.float32)
    summed_self, summed_neigh, summed_bias = lax.psum((self_term, neigh_term, bias_term), "dom")
    grad_self = scale * summed_self
    grad_neigh = scale * summed_neigh
    grad_bias = scale * summed_bias
    contract_last = (((1,), (1,)), ((), ()))
    grad_own = lax.dot_general(cotangent, w_self, contract_last, preferred_element_type=jnp.float32)
    d_agg = (
        lax.dot_general(cotangent, w_neigh, contract_last, preferred_element_type=jnp.float32)
        / floor
    ).astype(jnp.bfloat16)
    picked_back = jnp.einsum(
        "td,dif->tif",
        dst_pick,
        d_agg.reshape(dst_blocks, BLK, width),
        preferred_element_type=jnp.float32,
    ).astype(jnp.bfloat16)
    products_back = jnp.einsum(
        "tij,tif->tjf", masks, picked_back, preferred_element_type=jnp.float32
    )
    d_source = jnp.einsum(
        "tb,tjf->bjf",
        src_sum,
        products_back,
        precision=lax.Precision.HIGHEST,
        preferred_element_type=jnp.float32,
    ).reshape(-1, width)
    local_part = d_source[:rows_here]
    hub_part = d_source[rows_here : rows_here + hubs_total]
    edge_part = d_source[rows_here + hubs_total :].reshape(domains, send_rows, width)
    packed = jnp.concatenate([hub_part.reshape(domains, HUB_DEV, width), edge_part], axis=1)
    returned = lax.all_to_all(
        packed.astype(jnp.bfloat16), "dom", split_axis=0, concat_axis=0, tiled=True
    ).astype(packed.dtype)
    hub_back = jnp.sum(returned[:, :HUB_DEV], axis=0)
    edge_back = returned[:, HUB_DEV:]
    grads = grad_own + local_part
    grads = add_rows(grads, hub_list[0], hub_back)
    edge_live = jnp.where(live_send[:, :, None], edge_back, jnp.float32(0.0))
    grouped_values = edge_live.reshape(domains // group, group * send_rows, width)

    def add_group(total, inputs):
        indices, values = inputs
        return (add_rows(total, indices, values), None)

    grads, unused = lax.scan(add_group, grads, (grouped_lists, grouped_values))
    return (hidden_out, grads, grad_self, grad_neigh, grad_bias)


def solution(mesh):
    in_specs = (
        P("dom", "tile"),
        P("tile", None),
        P("tile", None),
        P(),
        P("dom", None),
        P("dom", None),
        P("dom", None, None),
        P("dom", None),
        P("dom", None),
        P("dom", None),
        P("dom"),
        P("dom", None, None, None),
    )
    out_specs = (P("dom", "tile"), P("dom", "tile"), P("tile", None), P("tile", None), P())
    return jax.shard_map(
        on_device, mesh=mesh, in_specs=in_specs, out_specs=out_specs, check_vma=False
    )
```

profile of v0, /device:TPU:2, one launch (start us, length us, event | category | flops | bytes accessed | tf_op | source)
XLA Modules:
  0.0 313.5 jit_solution(1332185316176799338)
XLA Ops:
  8.0 0.7 iota_compare_fusion.17
  8.8 0.9 reshape_squeeze.3
  9.7 32.3 %while.20 = (s32[]{:T(128)}, bf16[4,4096,32]{1,2,0:T(8,128)(2,1)S(1)}, s32[4,4096]{1,0:T(4,128)S(1)}, bf16[2048,32]{0,1:T(8,128)(2,1)}, s32[]{:T(128)}) while((s32[]{:T(128)}, bf16[4,4096,32]{1,2,0:T(8,128)(2,1)S(1)}, s32[4,4096]{1,0:T(4,128)S(1)}, bf16[2048,32]{0,1:T(8,128)(2,1)}, s32[]{:T(128)}) %tuple.40), condition=%wide.region_1.2_spmd, body=%wide.region_0.1_spmd.sunk | while | flops 545390592 | bytes 442437 | solution.py:55
  9.7 8.0 %fusion.85 = bf16[4,4096,32]{1,2,0:T(8,128)(2,1)S(1)} fusion(bf16[4,4096,32]{1,2,0:T(8,128)(2,1)S(1)} %get-tuple-element.142, s32[]{:T(128)} %get-tuple-element.141, bf16[2048,32]{0,1:T(8,128)(2,1)} %get-tuple-element.149, s32[4096]{0:T(1024)S(1)} %bitcast.105), kind=kOutput, calls=%fused_computation.5.clone.1 | convolution fusion | flops 545390592 | bytes 409604 | tf_op jit(solution)/shard_map/while/body/eval_jaxpr/dot_general | solution.py:16
  17.8 8.0 %fusion.85 = bf16[4,4096,32]{1,2,0:T(8,128)(2,1)S(1)} fusion(bf16[4,4096,32]{1,2,0:T(8,128)(2,1)S(1)} %get-tuple-element.142, s32[]{:T(128)} %get-tuple-element.141, bf16[2048,32]{0,1:T(8,128)(2,1)} %get-tuple-element.149, s32[4096]{0:T(1024)S(1)} %bitcast.105), kind=kOutput, calls=%fused_computation.5.clone.1 | convolution fusion | flops 545390592 | bytes 409604 | tf_op jit(solution)/shard_map/while/body/eval_jaxpr/dot_general | solution.py:16
  25.9 8.0 %fusion.85 = bf16[4,4096,32]{1,2,0:T(8,128)(2,1)S(1)} fusion(bf16[4,4096,32]{1,2,0:T(8,128)(2,1)S(1)} %get-tuple-element.142, s32[]{:T(128)} %get-tuple-element.141, bf16[2048,32]{0,1:T(8,128)(2,1)} %get-tuple-element.149, s32[4096]{0:T(1024)S(1)} %bitcast.105), kind=kOutput, calls=%fused_computation.5.clone.1 | convolution fusion | flops 545390592 | bytes 409604 | tf_op jit(solution)/shard_map/while/body/eval_jaxpr/dot_general | solution.py:16
  33.9 8.0 %fusion.85 = bf16[4,4096,32]{1,2,0:T(8,128)(2,1)S(1)} fusion(bf16[4,4096,32]{1,2,0:T(8,128)(2,1)S(1)} %get-tuple-element.142, s32[]{:T(128)} %get-tuple-element.141, bf16[2048,32]{0,1:T(8,128)(2,1)} %get-tuple-element.149, s32[4096]{0:T(1024)S(1)} %bitcast.105), kind=kOutput, calls=%fused_computation.5.clone.1 | convolution fusion | flops 545390592 | bytes 409604 | tf_op jit(solution)/shard_map/while/body/eval_jaxpr/dot_general | solution.py:16
  42.0 0.8 copy.36
  42.8 0.8 reshape.84
  43.7 1.5 copy.37
  45.3 12.3 %all-to-all-start = ((bf16[32,512,32]{1,2,0:T(8,128)(2,1)}), bf16[32,512,32]{1,2,0:T(8,128)(2,1)}, u32[]{:S(2)}, u32[]{:S(2)}) async-start(bf16[32,512,32]{1,2,0:T(8,128)(2,1)} %copy.37), calls=%async_computation | async-start | bytes 2097152 | tf_op jit(solution)/shard_map/all_to_all | solution.py:59
  58.3 6.5 %convert_reduce_fusion = f32[296,128]{1,0:T(8,128)S(1)} fusion(bf16[1,296,128,128]{3,2,1,0:T(8,128)(2,1)} %param.27), kind=kLoop, calls=%fused_computation.15 | loop fusion | flops 9661440 | bytes 9850880 | tf_op jit(solution)/shard_map/reduce_sum | solution.py:84
  65.6 1.5 convolution_convert_fusion
  67.1 1.3 reduce.1
  68.4 5.2 %fusion.26 = f32[296,128,32]{1,2,0:T(8,128)S(1)} fusion(bf16[1,296,128,128]{3,2,1,0:T(8,128)(2,1)} %param.27, bf16[296,128,32]{1,0,2:T(8,128)(2,1)S(1)} %convolution_convert_fusion), kind=kOutput, calls=%fused_computation.28 | convolution fusion | flops 310378496 | bytes 16973824 | tf_op jit(solution)/shard_map/tij,tif->tjf/dot_general | solution.py:125
  73.6 6.9 %fusion.61 = (bf16[148,128,32]{1,0,2:T(8,128)(2,1)S(1)}, f32[148,128,32]{1,0,2:T(8,128)}) fusion(f32[296,128,32]{1,2,0:T(8,128)S(1)} %fusion.26, s32[296]{0:T(512)S(1)} %copy-done.12, pred[296]{0:T(512)(128)(4,1)S(1)} %copy-done.15), kind=kOutput, calls=%fused_computation.76 | convolution fusion | flops 2153944576 | bytes 8488392 | tf_op jit(solution)/shard_map/tb,tjf->bjf/dot_general | solution.py:128
  80.9 0.7 reshape.90
  81.6 0.6 copy.46
  82.5 1.7 slice.28
  84.4 42.9 %all_gather.3 = bf16[512,32]{1,0:T(8,128)(2,1)S(1)} all-gather(bf16[16,32]{1,0:T(8,128)(2,1)S(1)} %convolution_convert_fusion.2), channel_id=1, replica_groups=mesh['dom'=32,'tile'=8] {'dom'}, dimensions={0}, use_global_device_ids=true | all-gather | bytes 33792 | tf_op jit(solution)/shard_map/all_gather | solution.py:58
  127.4 0.6 dynamic_slice.14
  128.0 1.8 pad_maximum_fusion
  129.8 0.8 convert_reduce_fusion.1
  130.7 0.9 fusion.63
  132.1 8.2 %all-to-all-start.1 = ((bf16[32,528,32]{1,2,0:T(8,128)(2,1)}), bf16[32,528,32]{1,2,0:T(8,128)(2,1)}, u32[]{:S(2)}, u32[]{:S(2)}) async-start(bf16[32,528,32]{1,2,0:T(8,128)(2,1)} %pad_maximum_fusion), calls=%async_computation.2 | async-start | bytes 2621440 | tf_op jit(solution)/shard_map/all_to_all | solution.py:139
  140.4 1.3 copy.50
  141.7 1.1 pad_maximum_fusion.1
  142.8 2.5 reshape.86
  145.3 2.1 convolution_convert_fusion.1
  147.5 7.6 %fusion.21 = f32[296,128,32]{1,2,0:T(8,128)S(1)} fusion(bf16[1,296,128,128]{3,2,1,0:T(8,128)(2,1)} %param.27, bf16[296,128,32]{1,0,2:T(8,128)(2,1)S(1)} %convolution_convert_fusion.1), kind=kOutput, calls=%fused_computation.27 | convolution fusion | flops 310378496 | bytes 16973824 | tf_op jit(solution)/shard_map/tij,tjf->tif/dot_general | solution.py:76
  155.2 4.5 %fusion.17 = f32[16,128,32]{1,0,2:T(8,128)S(1)} fusion(f32[296,128,32]{1,2,0:T(8,128)S(1)} %fusion.21, s32[296]{0:T(512)S(1)} %copy-done.9, pred[296]{0:T(512)(128)(4,1)S(1)} %copy-done.16), kind=kOutput, calls=%fused_computation.22 | convolution fusion | flops 232793344 | bytes 5113288 | tf_op jit(solution)/shard_map/td,tif->dif/dot_general | solution.py:77
  159.7 0.9 fusion.58
  160.7 1.9 convolution_add_fusion
  162.6 0.9 all-to-all-done.1
  163.4 1.7 copy_convert_fusion
  165.3 0.6 slice_select_fusion
  165.9 1.4 fusion.35
  167.3 4.7 %copy.49 = f32[32,512,32]{2,1,0:T(8,128)} copy(f32[32,512,32]{1,0,2:T(8,128)S(1)} %slice_select_fusion) | data formatting | bytes 4194304 | tf_op jit(solution)/shard_map/while | solution.py:153
  172.0 1.4 fusion.31
  173.3 71.8 %while.21 = (s32[]{:T(128)}, f32[2048,32]{0,1:T(8,128)S(1)}, s32[4,4096]{1,0:T(4,128)S(1)}, f32[4,4096,32]{2,1,0:T(8,128)}, s32[]{:T(128)}) while((s32[]{:T(128)}, f32[2048,32]{0,1:T(8,128)S(1)}, s32[4,4096]{1,0:T(4,128)S(1)}, f32[4,4096,32]{2,1,0:T(8,128)}, s32[]{:T(128)}) %tuple.52), condition=%wide.region_6.7_spmd, body=%wide.region_5.6_spmd.sunk | while | flops 3229679616 | bytes 2671169 | solution.py:153
  173.6 17.8 %fusion.87 = f32[2048,32]{0,1:T(8,128)S(1)} fusion(f32[2048,32]{0,1:T(8,128)S(1)} %get-tuple-element.157, s32[4096]{0:T(1024)S(1)} %bitcast.106, f32[4,4096,32]{2,1,0:T(8,128)} %get-tuple-element.164, s32[]{:T(128)} %get-tuple-element.156), kind=kOutput, calls=%fused_computation.10.clone.1 | convolution fusion | flops 3229679616 | bytes 2638336 | tf_op jit(solution)/shard_map/while/body/eval_jaxpr/dot_general | solution.py:23
  191.5 17.8 %fusion.87 = f32[2048,32]{0,1:T(8,128)S(1)} fusion(f32[2048,32]{0,1:T(8,128)S(1)} %get-tuple-element.157, s32[4096]{0:T(1024)S(1)} %bitcast.106, f32[4,4096,32]{2,1,0:T(8,128)} %get-tuple-element.164, s32[]{:T(128)} %get-tuple-element.156), kind=kOutput, calls=%fused_computation.10.clone.1 | convolution fusion | flops 3229679616 | bytes 2638336 | tf_op jit(solution)/shard_map/while/body/eval_jaxpr/dot_general | solution.py:23
  209.4 17.8 %fusion.87 = f32[2048,32]{0,1:T(8,128)S(1)} fusion(f32[2048,32]{0,1:T(8,128)S(1)} %get-tuple-element.157, s32[4096]{0:T(1024)S(1)} %bitcast.106, f32[4,4096,32]{2,1,0:T(8,128)} %get-tuple-element.164, s32[]{:T(128)} %get-tuple-element.156), kind=kOutput, calls=%fused_computation.10.clone.1 | convolution fusion | flops 3229679616 | bytes 2638336 | tf_op jit(solution)/shard_map/while/body/eval_jaxpr/dot_general | solution.py:23
  227.3 17.8 %fusion.87 = f32[2048,32]{0,1:T(8,128)S(1)} fusion(f32[2048,32]{0,1:T(8,128)S(1)} %get-tuple-element.157, s32[4096]{0:T(1024)S(1)} %bitcast.106, f32[4,4096,32]{2,1,0:T(8,128)} %get-tuple-element.164, s32[]{:T(128)} %get-tuple-element.156), kind=kOutput, calls=%fused_computation.10.clone.1 | convolution fusion | flops 3229679616 | bytes 2638336 | tf_op jit(solution)/shard_map/while/body/eval_jaxpr/dot_general | solution.py:23
  245.1 56.4 %all-reduce.3.cloned.1.call-done = (f32[32,256]{1,0:T(8,128)}, f32[32,256]{1,0:T(8,128)}, f32[256]{0:T(256)}) async-done(((f32[32,256]{1,0:T(8,128)}, f32[32,256]{1,0:T(8,128)}, f32[256]{0:T(256)}), (f32[32,256]{1,0:T(8,128)}, f32[32,256]{1,0:T(8,128)}, f32[256]{0:T(256)})) %all-reduce.3.cloned.1.call-update) | async-done | bytes 66576 | tf_op jit(solution)/shard_map/psum | solution.py:109
  301.5 1.2 broadcast_multiply_fusion.2
  302.8 1.4 broadcast_multiply_fusion
  304.2 1.7 add_convert_fusion
  (73 shorter events, 2.7 us)
Async XLA Ops:
  8.0 57.0 %copy-start = (bf16[32,256]{1,0:T(8,128)(2,1)S(1)}, bf16[32,256]{1,0:T(8,128)(2,1)}, u32[]{:S(2)}) copy-start(bf16[32,256]{1,0:T(8,128)(2,1)} %param.18) | copy-start | bytes 49156
  8.8 34.9 %copy-start.5 = (pred[32,512]{1,0:T(8,128)(4,1)}, pred[32,512]{1,0:T(8,128)(4,1)S(1)}, u32[]{:S(2)}) copy-start(pred[32,512]{1,0:T(8,128)(4,1)S(1)} %iota_compare_fusion.17) | copy-start | bytes 49156
  43.7 13.9 %copy-start.17 = (s32[1,296]{1,0:T(1,128)S(1)}, s32[1,296]{1,0:T(1,128)}, u32[]{:S(2)}) copy-start(s32[1,296]{1,0:T(1,128)} %param.24) | copy-start | bytes 3556
  45.3 86.8 %all-to-all-start = ((bf16[32,512,32]{1,2,0:T(8,128)(2,1)}), bf16[32,512,32]{1,2,0:T(8,128)(2,1)}, u32[]{:S(2)}, u32[]{:S(2)}) async-start(bf16[32,512,32]{1,2,0:T(8,128)(2,1)} %copy.37), calls=%async_computation | async-start | bytes 2097152 | tf_op jit(solution)/shard_map/all_to_all | solution.py:59
  57.6 7.1 %copy-start.8 = (s32[296]{0:T(512)}, s32[296]{0:T(512)S(1)}, u32[]{:S(2)}) copy-start(s32[296]{0:T(512)S(1)} %reduce) | copy-start | bytes 3556
  58.3 6.5 %copy-start.14 = (pred[296]{0:T(512)(128)(4,1)}, pred[296]{0:T(512)(128)(4,1)S(1)}, u32[]{:S(2)}) copy-start(pred[296]{0:T(512)(128)(4,1)S(1)} %iota_compare_fusion.19) | copy-start | bytes 892
  58.3 6.7 %copy-start.1 = (bf16[2048,256]{1,0:T(8,128)(2,1)S(1)}, bf16[2048,256]{1,0:T(8,128)(2,1)}, u32[]{:S(2)}) copy-start(bf16[2048,256]{1,0:T(8,128)(2,1)} %param.20) | copy-start | bytes 3145732
  65.0 0.6 copy-start.10
  68.4 5.2 %copy-start.12 = (s32[296]{0:T(512)S(1)}, s32[296]{0:T(512)}, u32[]{:S(2)}) copy-start(s32[296]{0:T(512)} %reduce.1) | copy-start | bytes 3556
  68.4 5.2 %copy-start.15 = (pred[296]{0:T(512)(128)(4,1)S(1)}, pred[296]{0:T(512)(128)(4,1)}, u32[]{:S(2)}) copy-start(pred[296]{0:T(512)(128)(4,1)} %copy-done.14) | copy-start | bytes 892
  80.9 3.3 %copy-start.2 = (bf16[2048,32]{0,1:T(8,128)(2,1)S(1)}, bf16[2048,32]{0,1:T(8,128)(2,1)}, u32[]{:S(2)}) copy-start(bf16[2048,32]{0,1:T(8,128)(2,1)} %get-tuple-element.177) | copy-start | bytes 393220
  80.9 3.3 %copy-start.18 = (s32[1,16]{1,0:T(1,128)S(1)}, s32[1,16]{1,0:T(1,128)}, u32[]{:S(2)}) copy-start(s32[1,16]{1,0:T(1,128)} %param.21) | copy-start | bytes 196
  80.9 46.5 %copy-start.21 = (f32[256]{0:T(256)S(1)}, f32[256]{0:T(256)}, u32[]{:S(2)}) copy-start(f32[256]{0:T(256)} %param.19) | copy-start | bytes 3076
  128.0 3.5 %copy-start.7 = (bf16[32,256]{1,0:T(8,128)(2,1)S(1)}, bf16[32,256]{1,0:T(8,128)(2,1)}, u32[]{:S(2)}) copy-start(bf16[32,256]{1,0:T(8,128)(2,1)} %param.17) | copy-start | bytes 49156
  132.1 31.3 %all-to-all-start.1 = ((bf16[32,528,32]{1,2,0:T(8,128)(2,1)}), bf16[32,528,32]{1,2,0:T(8,128)(2,1)}, u32[]{:S(2)}, u32[]{:S(2)}) async-start(bf16[32,528,32]{1,2,0:T(8,128)(2,1)} %pad_maximum_fusion), calls=%async_computation.2 | async-start | bytes 2621440 | tf_op jit(solution)/shard_map/all_to_all | solution.py:139
  140.3 161.2 %all-reduce.3.cloned.1.call-start = ((), (), s32[]{:S(2)}) async-start(), calls=%async_computation.4 | async-start | bytes 133120 | tf_op jit(solution)/shard_map/psum | solution.py:109
  141.7 3.6 %copy-start.13 = (s32[296]{0:T(512)S(1)}, s32[296]{0:T(512)}, u32[]{:S(2)}) copy-start(s32[296]{0:T(512)} %reduce.1) | copy-start | bytes 3556
  147.5 7.7 %copy-start.9 = (s32[296]{0:T(512)S(1)}, s32[296]{0:T(512)}, u32[]{:S(2)}) copy-start(s32[296]{0:T(512)} %copy-done.8) | copy-start | bytes 3556
  147.5 7.7 %copy-start.16 = (pred[296]{0:T(512)(128)(4,1)S(1)}, pred[296]{0:T(512)(128)(4,1)}, u32[]{:S(2)}) copy-start(pred[296]{0:T(512)(128)(4,1)} %copy-done.14) | copy-start | bytes 892
  155.2 4.5 %copy-start.11 = (f32[2048]{0:T(1024)S(1)}, f32[2048]{0:T(1024)}, u32[]{:S(2)}) copy-start(f32[2048]{0:T(1024)} %copy-done.10) | copy-start | bytes 24580
  160.6 143.5 %reduce-scatter.2.cloned.1.call-start = ((), (), s32[]{:S(2)}) async-start(), calls=%async_computation.3 | async-start | bytes 2359296 | tf_op jit(solution)/shard_map/reduce_scatter | solution.py:100
  162.6 2.7 copy-start.6
  165.2 0.7 copy-start.19
  167.3 4.7 %copy-start.3 = (f32[16,128,32]{1,0,2:T(8,128)S(1)}, f32[16,128,32]{1,0,2:T(8,128)}, u32[]{:S(2)}) copy-start(f32[16,128,32]{1,0,2:T(8,128)} %slice.28) | copy-start | bytes 786436
  173.3 130.8 %copy-start.20 = (f32[32]{0:T(128)S(1)}, f32[32]{0:T(128)}, u32[]{:S(2)}) copy-start(f32[32]{0:T(128)} %dynamic_slice.14) | copy-start | bytes 388
  245.1 60.7 %copy-start.4 = (f32[2048,32]{0,1:T(8,128)}, f32[2048,32]{0,1:T(8,128)S(1)}, u32[]{:S(2)}) copy-start(f32[2048,32]{0,1:T(8,128)S(1)} %get-tuple-element.45) | copy-start | bytes 786436
Sparse Core Ops, SparseCore 0:
  160.7 140.7 all-reduce.2
Sparse Core Ops, SparseCore 1:
  163.6 37.5 reduce-scatter.1
where the time goes:
time: 318 us; the launch traced here: 314 us
  matrix products  139 us (44%)
  waiting for transfers between devices  57.3 us (18%)
  blocking collectives  42.9 us (13%)
  starting transfers between devices  20.7 us (7%)
  other arithmetic  19 us (6%)
  local copies, waits for them, and re-layouts  17.3 us (5%)
  between operations  16.8 us (5%)
    dot_general x5, matrix products, add_rows(): jnp.dot(table, values, precision=lax.Precision.HIGHEST, preferred_element...  72.8 us
    psum x1, waiting for transfers between devices, on_device(): lax.psum((self_term, neigh_term, bias_term), 'dom')  56.4 us
    all_gather x1, blocking collectives, on_device(): hub_rows = lax.all_gather(own_hubs, 'dom', axis=0, tiled=True)  42.9 us
    dot_general x5, matrix products, select_rows(): jnp.dot(table, rows, preferred_element_type=jnp.float32).astype(rows.dtype)  32.4 us
    all_to_all x1, starting transfers between devices, on_device(): lax.all_to_all(outgoing, 'dom', split_axis=0, concat_axis=0, tiled=True)  12.3 us
    all_to_all x1, starting transfers between devices, on_device(): lax.all_to_all(packed.astype(jnp.bfloat16), 'dom', split_axis=0, concat_a...  8.25 us
    dot_general x1, matrix products, on_device(): jnp.einsum('tij,tjf->tif', masks, picked, preferred_element_type=jnp.floa...  7.65 us
    dot_general x1, matrix products, on_device(): jnp.einsum('tb,tjf->bjf', src_sum, products_back, precision=lax.Precision...  6.88 us
  transfers between devices with their start and end apart: 4, of which 2 were waited for; matrix products, arithmetic and copies ran while one was open for 44% of the time, Pallas kernels for 0%

commit v1 on v0

v1 whole, which is shorter than its diff:
```python
import functools
import math

import jax
import jax.numpy as jnp
from jax import lax
from jax.experimental import pallas as pl
from jax.experimental.pallas import tpu as pltpu
from jax.sharding import PartitionSpec as P

BLK = 128
HUB_DEV = 16
MESH = pl.DeviceIdType.MESH
F32 = jnp.float32
BF16 = jnp.bfloat16

N_DOM = 32
NX = 4
NZ = 8
NT = 8
ROWS = 2048
CH = 256
SEND = 512
OWN = ROWS // NT
HUBS = N_DOM * HUB_DEV
HUB0 = OWN
EDGE0 = OWN + HUBS
COLS = EDGE0 + 4 * SEND
RING = 16

DEG, WN, WS, FEAT, ACC, GRAD, AGG, HID = range(8)
FWD, BWD, HUBF, HUBB = range(4)


def nn(a, b):
    return jnp.dot(a, b, preferred_element_type=F32)


def nt(a, b):
    return lax.dot_general(a, b, (((1,), (1,)), ((), ())), preferred_element_type=F32)


def build_kernel(code_ref, mask_ref, a_ref, deg_ref, listed, ring, row_total, sems):
    cap = mask_ref.shape[0]

    def scan(t, n):
        listed[n] = t
        return n + (code_ref[t] >= 0).astype(jnp.int32)

    count = lax.fori_loop(0, cap, scan, jnp.int32(0))

    def fetch(i):
        slot = lax.rem(i, RING)
        return pltpu.make_async_copy(mask_ref.at[listed[i]], ring.at[slot], sems.at[slot])

    @pl.loop(0, jnp.minimum(count, RING))
    def _(i):
        fetch(i).start()

    @pl.loop(0, ROWS // 64)
    def _(r):
        start = pl.multiple_of(r * 64, 64)
        a_ref[pl.ds(start, 64), :] = jnp.zeros((64, COLS), BF16)
        row_total[pl.ds(start, 64), :] = jnp.zeros((64, BLK), F32)

    @pl.loop(0, count)
    def _(i):
        fetch(i).wait()
        code = code_ref[listed[i]]
        tile = ring[lax.rem(i, RING)]
        dst = pl.ds(pl.multiple_of((code // 64) * BLK, BLK), BLK)
        col = pl.ds(pl.multiple_of((lax.rem(code, 64) // 2) * BLK, BLK), BLK)
        a_ref[dst, col] = a_ref[dst, col] + tile
        row_total[dst, :] = row_total[dst, :] + tile.astype(F32) * lax.rem(code, 2).astype(F32)

        @pl.when(i + RING < count)
        def _():
            fetch(i + RING).start()

    ones = jnp.ones((8, BLK), F32)
    for d in range(ROWS // BLK):
        sums = lax.dot_general(
            ones,
            row_total[d * BLK : (d + 1) * BLK, :],
            (((1,), (1,)), ((), ())),
            precision=lax.Precision.HIGHEST,
            preferred_element_type=F32,
        )
        deg_ref[d : d + 1, :] = sums[0:1, :]


def build_adjacency(codes, masks):
    return pl.pallas_call(
        build_kernel,
        out_shape=(
            jax.ShapeDtypeStruct((ROWS, COLS), BF16),
            jax.ShapeDtypeStruct((ROWS // BLK, BLK), F32),
        ),
        in_specs=[
            pl.BlockSpec(memory_space=pltpu.SMEM),
            pl.BlockSpec(memory_space=pl.ANY),
        ],
        out_specs=(
            pl.BlockSpec(memory_space=pltpu.VMEM),
            pl.BlockSpec(memory_space=pltpu.VMEM),
        ),
        scratch_shapes=[
            pltpu.SMEM((masks.shape[0] + 1,), jnp.int32),
            pltpu.VMEM((RING, BLK, BLK), BF16),
            pltpu.VMEM((ROWS, BLK), F32),
            pltpu.SemaphoreType.DMA((RING,)),
        ],
        compiler_params=pltpu.CompilerParams(vmem_limit_bytes=40 * 2**20),
        name="adjacency",
    )(codes, masks)


def layer_kernel(
    feat_ref,
    ws_ref,
    wn_ref,
    bias_ref,
    cot_ref,
    hub_ref,
    send_ref,
    count_ref,
    a_hbm,
    deg_ref,
    hid_out,
    grad_out,
    gself_out,
    gneigh_out,
    gbias_out,
    feat,
    ws,
    wn,
    degs,
    adj,
    pick,
    hub_pick,
    fsend,
    frecv,
    bsend,
    brecv,
    hfs,
    hfr,
    hub_src,
    hbs,
    hbr,
    dagg,
    acc,
    grads,
    acc_send,
    acc_recv,
    grad_send,
    grad_recv,
    agg_send,
    agg_recv,
    hid_send,
    hid_recv,
    wgrad,
    xsend,
    xrecv,
    zsend,
    zrecv,
    gsend,
    grecv,
    local_sem,
    tss,
    trs,
    jss,
    jrs,
    xss,
    xrs,
    zss,
    zrs,
    gss,
    grs,
):
    me = lax.axis_index("dom")
    j = lax.axis_index("tile")
    z, x = me // NX, lax.rem(me, NX)
    y, core = j // 2, lax.rem(j, 2)
    scale = 1.0 / math.sqrt(N_DOM * ROWS)

    load_adj = pltpu.make_async_copy(a_hbm, adj, local_sem.at[0])
    load_adj.start()

    def peer(d):
        return (me, lax.rem(j + d, NT))

    def at_x(d):
        return (z * NX + lax.rem(x + d, NX), j)

    def at_z(d):
        return (lax.rem(z + d, NZ) * NX + x, j)

    def to_dom(k):
        return lax.rem(z + j - 2 * k + 2 * NZ, NZ) * NX + lax.rem(x + k, NX)

    def from_dom(k):
        return lax.rem(z - j + 2 * k + 2 * NZ, NZ) * NX + lax.rem(x - k + NX, NX)

    barrier = pltpu.get_barrier_semaphore()

    def greet(device):
        pl.semaphore_signal(barrier, inc=1, device_id=device, device_id_type=MESH)

    for d in range(1, NT):
        greet(peer(d))
    for d in range(1, NX):
        greet(at_x(d))
    for d in range(1, NZ):
        greet(at_z(d))
    for k in range(1, 4):
        greet((to_dom(k), j))
        greet((from_dom(k), j))

    @pl.when(j != 0)
    def _():
        greet((to_dom(0), j))
        greet((from_dom(0), j))

    pl.semaphore_wait(barrier, 23 + 2 * (j != 0).astype(jnp.int32))

    def tile_copy(cat, d, src, dst, device):
        return pltpu.make_async_remote_copy(
            src_ref=src,
            dst_ref=dst,
            send_sem=tss.at[cat, d],
            recv_sem=trs.at[cat, d],
            device_id=device,
            device_id_type=MESH,
        )

    def rows32(index):
        return pl.ds(pl.multiple_of(index * 32, 32), 32)

    sent = []

    deg_copies, weight_copies = [], []
    for d in range(1, NT):
        c = tile_copy(DEG, d, deg_ref, degs.at[d], peer(d))
        c.start()
        deg_copies.append(c)
    for d in range(1, NT):
        c = tile_copy(WN, d, wn_ref, wn.at[rows32(j)], peer(d))
        c.start()
        weight_copies.append(c)
    feat_copies = {}
    for d in (1, 3, 2):
        c = tile_copy(FEAT, d, feat_ref, feat.at[rows32(j)], (me, lax.rem(j + 2 * d, NT)))
        c.start()
        feat_copies[d] = c
    partner = (me, j + 1 - 2 * core)
    c = tile_copy(FEAT, 0, feat_ref, feat.at[rows32(j)], partner)
    c.start()
    feat_copies[0] = c
    for d in range(1, NT):
        c = tile_copy(WS, d, ws_ref, ws.at[rows32(j)], peer(d))
        c.start()
        weight_copies.append(c)

    feat[rows32(j), :] = feat_ref[...]
    wn[rows32(j), :] = wn_ref[...]
    ws[rows32(j), :] = ws_ref[...]

    lanes = lax.broadcasted_iota(jnp.int32, (1, SEND), 1)
    for k in range(4):
        q = to_dom(k)
        index = jnp.where(lanes < count_ref[0, q], send_ref[0, pl.ds(q, 1), :], -1)

        @pl.loop(0, ROWS // 128)
        def _(r):
            base = pl.multiple_of(r * 128, 128)
            row = lax.broadcasted_iota(jnp.int32, (128, SEND), 0) + base
            pick[k, pl.ds(base, 128), :] = (row == index).astype(F32).astype(BF16)

    slot = lax.broadcasted_iota(jnp.int32, (HUB_DEV, BLK), 0)
    hub_index = jnp.zeros((HUB_DEV, BLK), jnp.int32)
    for i in range(HUB_DEV):
        hub_index = jnp.where(slot == i, hub_ref[0, i], hub_index)
    for r in range(ROWS // BLK):
        column = lax.broadcasted_iota(jnp.int32, (HUB_DEV, BLK), 1) + r * BLK
        hub_pick[:, r * BLK : (r + 1) * BLK] = (column == hub_index).astype(F32).astype(BF16)

    for c in deg_copies:
        c.wait_recv()
    degree = deg_ref[...]
    for d in range(1, NT):
        degree = degree + degs[d]
    degs[0] = jnp.maximum(degree, 1.0)
    for c in weight_copies[: NT - 1]:
        c.wait_recv()

    @pl.loop(0, ROWS // 256)
    def _(r):
        start = pl.multiple_of(r * 256, 256)
        part = nt(wn[...], cot_ref[pl.ds(start, 256), :])
        for h in range(2):
            floor = degs[0, pl.ds(2 * r + h, 1), :]
            dagg[:, pl.ds(start + h * BLK, BLK)] = (
                part[:, h * BLK : (h + 1) * BLK] / floor
            ).astype(BF16)

    load_adj.wait()

    def dom_copy(cat, k, src, dst, device):
        return pltpu.make_async_remote_copy(
            src_ref=src,
            dst_ref=dst,
            send_sem=jss.at[cat, k],
            recv_sem=jrs.at[cat, k],
            device_id=(device, j),
            device_id_type=MESH,
        )

    def dom_start(cat, k, src, dst, device):
        copy = dom_copy(cat, k, src, dst, device)
        if k == 0:

            @pl.when(j != 0)
            def _():
                copy.start()

            @pl.when(j == 0)
            def _():
                pltpu.make_async_copy(src, dst, jrs.at[cat, k]).start()
        else:
            copy.start()
        return copy

    dom_copies = {}
    for k in (3, 2, 1, 0):

        @pl.loop(0, SEND // 256)
        def _(h):
            col = pl.multiple_of(EDGE0 + k * SEND + h * 256, 256)
            bsend[k, :, pl.ds(pl.multiple_of(h * 256, 256), 256)] = nn(
                dagg[...], adj[:, pl.ds(col, 256)]
            ).astype(BF16)

        dom_copies[BWD, k] = dom_start(BWD, k, bsend.at[k], brecv.at[k], from_dom(k))

    @pl.loop(0, HUBS // 256)
    def _(h):
        col = pl.multiple_of(HUB0 + h * 256, 256)
        part = nn(dagg[...], adj[:, pl.ds(col, 256)])
        hbs[pl.ds(pl.multiple_of(h * 256, 256), 256), :] = part.T.astype(BF16)

    for k in range(4):
        rows = pl.ds(pl.multiple_of(from_dom(k) * HUB_DEV, HUB_DEV), HUB_DEV)
        dom_copies[HUBB, k] = dom_start(HUBB, k, hbs.at[rows], hbr.at[k], from_dom(k))

    for d in (1, 3, 2):
        feat_copies[d].wait_recv()
        owner = 2 * lax.rem(y - d + 4, 4) + core
        c = tile_copy(FEAT, 4 + d, feat.at[rows32(owner)], feat.at[rows32(owner)], partner)
        c.start()
        feat_copies[4 + d] = c
    feat_copies[0].wait_recv()
    for d in (1, 3, 2):
        feat_copies[4 + d].wait_recv()

    hfs[...] = nt(hub_pick[...], feat[...]).astype(BF16)
    for k in range(4):
        dom_copies[HUBF, k] = dom_start(HUBF, k, hfs, hfr.at[k], to_dom(k))
    for k in (3, 2, 1, 0):

        @pl.loop(0, SEND // 256)
        def _(h):
            cols = pl.ds(pl.multiple_of(h * 256, 256), 256)
            fsend[k, :, cols] = nn(feat[...], pick[k, :, cols]).astype(BF16)

        dom_copies[FWD, k] = dom_start(FWD, k, fsend.at[k], frecv.at[k], to_dom(k))

    own = pl.ds(pl.multiple_of(j * OWN, OWN), OWN)

    @pl.loop(0, ROWS // 256)
    def _(r):
        rows = pl.ds(pl.multiple_of(r * 256, 256), 256)
        acc[:, rows] = nt(feat[:, own], adj[rows, 0:OWN])
        grads[:, rows] = jnp.zeros((CH, 256), F32)
        grad_out[:, rows] = nt(ws_ref[...], cot_ref[rows, :])

    grads[:, own] = nn(dagg[...], adj[:, 0:OWN])
    wgrad[0:32, :] = nn(feat_ref[...], cot_ref[...])
    wgrad[64:72, :] = nn(jnp.ones((8, ROWS), BF16), cot_ref[...])

    for k in (3, 2, 1, 0):
        dom_copies[BWD, k].wait_recv()

        @pl.loop(0, ROWS // 256)
        def _(r):
            rows = pl.ds(pl.multiple_of(r * 256, 256), 256)
            grads[:, rows] = grads[:, rows] + nt(brecv[k], pick[k, rows, :])

    for k in range(4):
        dom_copies[HUBB, k].wait_recv()
    hub_back = jnp.concatenate([hbr[k].astype(F32) for k in range(4)], axis=0)
    hub_back = jnp.concatenate([hub_back, jnp.zeros_like(hub_back)], axis=0).T.astype(BF16)

    @pl.loop(0, ROWS // 256)
    def _(r):
        rows = pl.ds(pl.multiple_of(r * 256, 256), 256)
        table = jnp.concatenate([hub_pick[:, rows]] * 8, axis=0)
        grads[:, rows] = grads[:, rows] + nn(hub_back, table)
        grad_send[:, rows] = grads[:, rows].astype(BF16)

    grad_copies = []
    for d in range(1, NT):
        c = tile_copy(
            GRAD, d, grad_send.at[rows32(lax.rem(j + d, NT))], grad_recv.at[d], peer(d)
        )
        c.start()
        grad_copies.append(c)

    for k in range(4):
        dom_copies[HUBF, k].wait_recv()
    hub_src[...] = jnp.zeros((HUBS, CH), BF16)
    for k in range(4):
        rows = pl.ds(pl.multiple_of(from_dom(k) * HUB_DEV, HUB_DEV), HUB_DEV)
        hub_src[rows, :] = hfr[k]
    hub_src_t = hub_src[...].astype(F32).T.astype(BF16)

    @pl.loop(0, ROWS // 256)
    def _(r):
        rows = pl.ds(pl.multiple_of(r * 256, 256), 256)
        acc[:, rows] = acc[:, rows] + nt(hub_src_t, adj[rows, HUB0:EDGE0])

    for k in (3, 2, 1, 0):
        dom_copies[FWD, k].wait_recv()

        @pl.loop(0, ROWS // 256)
        def _(r):
            rows = pl.ds(pl.multiple_of(r * 256, 256), 256)
            acc[:, rows] = acc[:, rows] + nt(
                frecv[k], adj[rows, EDGE0 + k * SEND : EDGE0 + (k + 1) * SEND]
            )

    @pl.loop(0, NT)
    def _(r):
        rows = pl.ds(pl.multiple_of(r * 256, 256), 256)
        acc_send[r] = acc[:, rows].astype(BF16)

    acc_copies = []
    for d in range(1, NT):
        c = tile_copy(ACC, d, acc_send.at[lax.rem(j + d, NT)], acc_recv.at[d], peer(d))
        c.start()
        acc_copies.append(c)

    for c in grad_copies:
        c.wait_recv()
    total = grads[rows32(j), :]
    for d in range(1, NT):
        total = total + grad_recv[d].astype(F32)
    grad_out[...] = grad_out[...] + total

    for c in weight_copies[NT - 1 :]:
        c.wait_recv()
    ws_t = ws[...].astype(F32).T.astype(BF16)
    wn_t = wn[...].astype(F32).T.astype(BF16)
    bias_t = jnp.broadcast_to(bias_ref[...], (BLK, CH)).T
    mixed = nn(ws_t, feat[:, own])
    for c in acc_copies:
        c.wait_recv()
    total = acc[:, own]
    for d in range(1, NT):
        total = total + acc_recv[d].astype(F32)
    for h in range(2):
        cols = slice(h * BLK, (h + 1) * BLK)
        floor = degs[0, pl.ds(2 * j + h, 1), :]
        agg_send[:, cols] = (total[:, cols] / floor).astype(BF16)
    agg_copies = []
    for d in range(1, NT):
        c = tile_copy(
            AGG, d, agg_send.at[rows32(lax.rem(j + d, NT))], agg_recv.at[:, own], peer(d)
        )
        c.start()
        agg_copies.append(c)
    agg_recv[:, own] = agg_send[rows32(j), :]
    mixed = mixed + nn(wn_t, agg_send[...])
    for h in range(2):
        cols = slice(h * BLK, (h + 1) * BLK)
        hid_send[:, cols] = (mixed[:, cols] + bias_t).astype(BF16)
    hid_copies = []
    for d in range(1, NT):
        c = tile_copy(
            HID, d, hid_send.at[rows32(lax.rem(j + d, NT))], hid_recv.at[:, own], peer(d)
        )
        c.start()
        hid_copies.append(c)
    hid_recv[:, own] = hid_send[rows32(j), :]

    for c in agg_copies:
        c.wait_recv()
    wgrad[32:64, :] = nn(agg_recv[...], cot_ref[...])

    def chunk(index):
        return pl.ds(pl.multiple_of(index * 8, 8), 8)

    for d in range(NX):
        to = lax.rem(x + d, NX)
        xsend[d, 0:8, :] = wgrad[chunk(to), :]
        xsend[d, 8:16, :] = wgrad[chunk(4 + to), :]
        xsend[d, 16:24, :] = wgrad[64:72, :]
    x_copies = []
    for d in range(1, NX):
        c = pltpu.make_async_remote_copy(
            src_ref=xsend.at[d],
            dst_ref=xrecv.at[x],
            send_sem=xss.at[d],
            recv_sem=xrs.at[d],
            device_id=at_x(d),
            device_id_type=MESH,
        )
        c.start()
        x_copies.append(c)
    xrecv[x] = xsend[0]
    for c in x_copies:
        c.wait_recv()
    total = xrecv[0]
    for d in range(1, NX):
        total = total + xrecv[d]
    zsend[...] = total
    z_copies = []
    for d in range(1, NZ):
        c = pltpu.make_async_remote_copy(
            src_ref=zsend,
            dst_ref=zrecv.at[z],
            send_sem=zss.at[d],
            recv_sem=zrs.at[d],
            device_id=at_z(d),
            device_id_type=MESH,
        )
        c.start()
        z_copies.append(c)
    zrecv[z] = zsend[...]
    for c in z_copies:
        c.wait_recv()
    total = zrecv[0]
    for d in range(1, NZ):
        total = total + zrecv[d]
    total = total * scale
    gsend[...] = total[0:16, :]
    gbias_out[...] = total[16:17, :]
    g_copies = []
    for d in range(1, NX):
        c = pltpu.make_async_remote_copy(
            src_ref=gsend,
            dst_ref=grecv.at[d],
            send_sem=gss.at[d],
            recv_sem=grs.at[d],
            device_id=at_x(d),
            device_id_type=MESH,
        )
        c.start()
        g_copies.append(c)
    gself_out[chunk(x), :] = gsend[0:8, :]
    gneigh_out[chunk(x), :] = gsend[8:16, :]

    for c in hid_copies:
        c.wait_recv()
    hid_out[...] = hid_recv[...]

    for d in range(1, NX):
        g_copies[d - 1].wait_recv()
        origin = lax.rem(x - d + NX, NX)
        gself_out[chunk(origin), :] = grecv[d, 0:8, :]
        gneigh_out[chunk(origin), :] = grecv[d, 8:16, :]

    groups = (deg_copies, weight_copies, list(feat_copies.values()), grad_copies, acc_copies)
    for group in groups + (agg_copies, hid_copies, x_copies, z_copies, g_copies):
        for c in group:
            c.wait_send()
    for (cat, k), c in dom_copies.items():
        if k == 0:

            @pl.when(j != 0)
            def _():
                c.wait_send()
        else:
            c.wait_send()


def run_layer(feat_t, w_self, w_neigh, bias, cot, hubs, sends, counts, adjacency, degree):
    vmem = pl.BlockSpec(memory_space=pltpu.VMEM)
    smem = pl.BlockSpec(memory_space=pltpu.SMEM)
    dma = pltpu.SemaphoreType.DMA
    return pl.pallas_call(
        layer_kernel,
        out_shape=(
            jax.ShapeDtypeStruct((32, ROWS), BF16),
            jax.ShapeDtypeStruct((32, ROWS), F32),
            jax.ShapeDtypeStruct((32, CH), F32),
            jax.ShapeDtypeStruct((32, CH), F32),
            jax.ShapeDtypeStruct((1, CH), F32),
        ),
        in_specs=[vmem, vmem, vmem, vmem, vmem, smem, vmem, smem]
        + [pl.BlockSpec(memory_space=pl.ANY), vmem],
        out_specs=(vmem,) * 5,
        scratch_shapes=[
            pltpu.VMEM((CH, ROWS), BF16),
            pltpu.VMEM((CH, CH), BF16),
            pltpu.VMEM((CH, CH), BF16),
            pltpu.VMEM((NT, ROWS // BLK, BLK), F32),
            pltpu.VMEM((ROWS, COLS), BF16),
            pltpu.VMEM((4, ROWS, SEND), BF16),
            pltpu.VMEM((HUB_DEV, ROWS), BF16),
            pltpu.VMEM((4, CH, SEND), BF16),
            pltpu.VMEM((4, CH, SEND), BF16),
            pltpu.VMEM((4, CH, SEND), BF16),
            pltpu.VMEM((4, CH, SEND), BF16),
            pltpu.VMEM((HUB_DEV, CH), BF16),
            pltpu.VMEM((4, HUB_DEV, CH), BF16),
            pltpu.VMEM((HUBS, CH), BF16),
            pltpu.VMEM((HUBS, CH), BF16),
            pltpu.VMEM((4, HUB_DEV, CH), BF16),
            pltpu.VMEM((CH, ROWS), BF16),
            pltpu.VMEM((CH, ROWS), F32),
            pltpu.VMEM((CH, ROWS), F32),
            pltpu.VMEM((NT, CH, OWN), BF16),
            pltpu.VMEM((NT, CH, OWN), BF16),
            pltpu.VMEM((CH, ROWS), BF16),
            pltpu.VMEM((NT, 32, ROWS), BF16),
            pltpu.VMEM((CH, OWN), BF16),
            pltpu.VMEM((32, ROWS), BF16),
            pltpu.VMEM((CH, OWN), BF16),
            pltpu.VMEM((32, ROWS), BF16),
            pltpu.VMEM((72, CH), F32),
            pltpu.VMEM((NX, 24, CH), F32),
            pltpu.VMEM((NX, 24, CH), F32),
            pltpu.VMEM((24, CH), F32),
            pltpu.VMEM((NZ, 24, CH), F32),
            pltpu.VMEM((16, CH), F32),
            pltpu.VMEM((NX, 16, CH), F32),
            dma((1,)),
            dma((8, NT)),
            dma((8, NT)),
            dma((4, 4)),
            dma((4, 4)),
            dma((NX,)),
            dma((NX,)),
            dma((NZ,)),
            dma((NZ,)),
            dma((NX,)),
            dma((NX,)),
        ],
        compiler_params=pltpu.CompilerParams(
            collective_id=0, has_side_effects=True, vmem_limit_bytes=56 * 2**20
        ),
        name="layer",
    )(feat_t, w_self, w_neigh, bias, cot, hubs, sends, counts, adjacency, degree)


def on_device(
    features,
    w_self,
    w_neigh,
    bias,
    cotangent,
    hub_list,
    send_list,
    send_count,
    tile_dst,
    tile_src,
    tile_count,
    tile_mask,
):
    me = lax.axis_index("dom")
    j = lax.axis_index("tile")
    z, x = me // NX, me % NX

    src, dst = tile_src[0], tile_dst[0]
    live = jnp.arange(src.shape[0], dtype=jnp.int32) < tile_count[0]
    own_blocks, hub_blocks = ROWS // BLK, HUBS // BLK
    edge = src - own_blocks - hub_blocks
    sender = edge // (SEND // BLK)
    k = (x - sender) % NX
    edge_owner = (z - sender // NX + 2 * k) % NZ
    is_own = src < own_blocks
    is_hub = jnp.logical_not(is_own) & (edge < 0)
    mine = jnp.where(is_own, src // (OWN // BLK) == j, is_hub | (edge_owner == j))
    slot = jnp.where(
        is_own,
        src % (OWN // BLK),
        jnp.where(
            is_hub,
            src - own_blocks + HUB0 // BLK,
            EDGE0 // BLK + k * (SEND // BLK) + edge % (SEND // BLK),
        ),
    )
    counted = jnp.where(is_hub & (j != 0), 0, 1)
    codes = jnp.where(live & mine, dst * 64 + slot * 2 + counted, -1).astype(jnp.int32)

    adjacency, degree = build_adjacency(codes, tile_mask[0])
    hidden_t, grad_t, grad_self, grad_neigh, grad_bias = run_layer(
        features.T,
        w_self,
        w_neigh,
        bias[None, :],
        cotangent,
        hub_list,
        send_list,
        send_count,
        adjacency,
        degree,
    )
    return (hidden_t.T, grad_t.T, grad_self, grad_neigh, grad_bias[0])


def solution(mesh):
    in_specs = (
        P("dom", "tile"),
        P("tile", None),
        P("tile", None),
        P(),
        P("dom", None),
        P("dom", None),
        P("dom", None, None),
        P("dom", None),
        P("dom", None),
        P("dom", None),
        P("dom"),
        P("dom", None, None, None),
    )
    out_specs = (P("dom", "tile"), P("dom", "tile"), P("tile", None), P("tile", None), P())
    return jax.shard_map(
        on_device, mesh=mesh, in_specs=in_specs, out_specs=out_specs, check_vma=False
    )
```

time: 318 us -> 134 us (0.42)
  the two profiles are of different devices: /device:TPU:2 before, /device:TPU:1 now
where the time goes in v1:
time: 134 us; the launch traced here: 133 us
  Pallas kernels  119 us (89%)
  local copies, waits for them, and re-layouts  11.5 us (9%)
  other arithmetic  1.43 us (1%)
  between operations  1.34 us (1%)
    pallas_call x1, Pallas kernels, run_layer(): pl.pallas_call(layer_kernel, out_shape=(jax.ShapeDtypeStruct((32, ROWS),...  109 us
    unnamed x9, local copies, waits for them, and re-layouts  11.5 us
    pallas_call x1, Pallas kernels, build_adjacency(): pl.pallas_call(build_kernel, out_shape=(jax.ShapeDtypeStruct((ROWS, COLS)...  9.85 us

profile of v1, /device:TPU:1, one launch (start us, length us, event | category | flops | bytes accessed | tf_op | source)
XLA Modules:
  0.0 133.5 jit_solution(240627901418516531)
XLA Ops:
  1.3 0.7 multiply_reduce_fusion
  2.0 0.7 reduce
  2.7 0.0 copy-start
  2.8 3.7 %copy-done = bf16[1,296,128,128]{3,2,1,0:T(8,128)(2,1)S(1)} copy-done((bf16[1,296,128,128]{3,2,1,0:T(8,128)(2,1)S(1)}, bf16[1,296,128,128]{3,2,1,0:T(8,128)(2,1)}, u32[]{:S(2)}) %copy-start) | copy-done | bytes 9699352
  6.5 9.9 %adjacency.1 = (bf16[2048,2816]{1,0:T(8,128)(2,1)}, f32[16,128]{1,0:T(8,128)S(1)}) custom-call(s32[296]{0:T(512)S(1)} %fusion.11.code_ref, bf16[296,128,128]{2,1,0:T(8,128)(2,1)S(1)} %bitcast.8), custom_call_target="tpu_custom_call" | custom-call | tf_op jit(solution)/shard_map/adjacency/pallas_call | solution.py:93
  16.4 0.0 copy-start.1
  16.4 0.6 copy-done.1
  17.0 109.3 %layer.1 = (bf16[32,2048]{1,0:T(8,128)(2,1)}, f32[32,2048]{1,0:T(8,128)}, f32[32,256]{1,0:T(8,128)}, f32[32,256]{1,0:T(8,128)}, f32[1,256]{1,0:T(1,128)}) custom-call(bf16[32,2048]{1,0:T(8,128)(2,1)} %bitcast.10, bf16[32,256]{1,0:T(8,128)(2,1)} %ws_ref.1, bf16[32,256]{1,0:T(8,128)(2,1)} %wn_ref.1, f32[1,256]{1,0:T(1,128)} %bitcast.12, ...), custom_call_target="tpu_custom_call" | custom-call | tf_op jit(solution)/shard_map/layer/pallas_call | solution.py:590
  126.3 1.6 %copy.23 = bf16[2048,32]{0,1:T(8,128)(2,1)} copy(bf16[2048,32]{0,1:T(8,128)(2,1)} %bitcast.11) | data formatting | bytes 262144
  127.9 1.7 %copy.24 = f32[2048,32]{0,1:T(8,128)} copy(f32[2048,32]{0,1:T(8,128)} %bitcast.9) | data formatting | bytes 524288
  129.6 1.4 %copy.25 = f32[32,256]{1,0:T(8,128)} copy(f32[32,256]{1,0:T(8,128)} %get-tuple-element.26) | data formatting | bytes 65536
  130.9 1.4 %copy.26 = f32[32,256]{1,0:T(8,128)} copy(f32[32,256]{1,0:T(8,128)} %get-tuple-element.27) | data formatting | bytes 65536
  132.3 1.2 copy.27
  (1 shorter events, 0.0 us)
Async XLA Ops:
  2.7 3.8 %copy-start = (bf16[1,296,128,128]{3,2,1,0:T(8,128)(2,1)S(1)}, bf16[1,296,128,128]{3,2,1,0:T(8,128)(2,1)}, u32[]{:S(2)}) copy-start(bf16[1,296,128,128]{3,2,1,0:T(8,128)(2,1)} %param.23) | copy-start | bytes 29097988
  16.4 0.6 copy-start.1

commit v2 on v1

--- a/solution.py
+++ b/solution.py
@@ -110,7 +110,7 @@
             pltpu.VMEM((ROWS, BLK), F32),
             pltpu.SemaphoreType.DMA((RING,)),
         ],
-        compiler_params=pltpu.CompilerParams(vmem_limit_bytes=40 * 2**20),
+        compiler_params=pltpu.CompilerParams(vmem_limit_bytes=60 * 2**20),
         name="adjacency",
     )(codes, masks)
 
@@ -150,10 +150,15 @@
     dagg,
     acc,
     grads,
+    acc_pair,
     acc_send,
     acc_recv,
+    grad_pair_send,
+    grad_pair,
     grad_send,
     grad_recv,
+    mixed,
+    wn_t,
     agg_send,
     agg_recv,
     hid_send,
@@ -233,11 +238,22 @@
             device_id_type=MESH,
         )
 
+    partner = (me, j + 1 - 2 * core)
+
+    def at_y(d):
+        return (me, 2 * lax.rem(y + d, 4) + core)
+
     def rows32(index):
         return pl.ds(pl.multiple_of(index * 32, 32), 32)
 
-    sent = []
-
+    feat_copies = {}
+    for d in (1, 3, 2):
+        c = tile_copy(FEAT, d, feat_ref, feat.at[rows32(j)], at_y(d))
+        c.start()
+        feat_copies[d] = c
+    c = tile_copy(FEAT, 0, feat_ref, feat.at[rows32(j)], partner)
+    c.start()
+    feat_copies[0] = c
     deg_copies, weight_copies = [], []
     for d in range(1, NT):
         c = tile_copy(DEG, d, deg_ref, degs.at[d], peer(d))
@@ -247,15 +263,6 @@
         c = tile_copy(WN, d, wn_ref, wn.at[rows32(j)], peer(d))
         c.start()
         weight_copies.append(c)
-    feat_copies = {}
-    for d in (1, 3, 2):
-        c = tile_copy(FEAT, d, feat_ref, feat.at[rows32(j)], (me, lax.rem(j + 2 * d, NT)))
-        c.start()
-        feat_copies[d] = c
-    partner = (me, j + 1 - 2 * core)
-    c = tile_copy(FEAT, 0, feat_ref, feat.at[rows32(j)], partner)
-    c.start()
-    feat_copies[0] = c
     for d in range(1, NT):
         c = tile_copy(WS, d, ws_ref, ws.at[rows32(j)], peer(d))
         c.start()
@@ -283,6 +290,16 @@
     for r in range(ROWS // BLK):
         column = lax.broadcasted_iota(jnp.int32, (HUB_DEV, BLK), 1) + r * BLK
         hub_pick[:, r * BLK : (r + 1) * BLK] = (column == hub_index).astype(F32).astype(BF16)
+
+    def relay(d):
+        feat_copies[d].wait_recv()
+        owner = 2 * lax.rem(y - d + 4, 4) + core
+        c = tile_copy(FEAT, 4 + d, feat.at[rows32(owner)], feat.at[rows32(owner)], partner)
+        c.start()
+        feat_copies[4 + d] = c
+
+    relay(1)
+    relay(3)
 
     for c in deg_copies:
         c.wait_recv()
@@ -303,6 +320,7 @@
                 part[:, h * BLK : (h + 1) * BLK] / floor
             ).astype(BF16)
 
+    relay(2)
     load_adj.wait()
 
     def dom_copy(cat, k, src, dst, device):
@@ -331,8 +349,8 @@
         return copy
 
     dom_copies = {}
-    for k in (3, 2, 1, 0):
-
+
+    def send_back(k):
         @pl.loop(0, SEND // 256)
         def _(h):
             col = pl.multiple_of(EDGE0 + k * SEND + h * 256, 256)
@@ -342,6 +360,28 @@
 
         dom_copies[BWD, k] = dom_start(BWD, k, bsend.at[k], brecv.at[k], from_dom(k))
 
+    send_back(3)
+
+    feat_copies[0].wait_recv()
+    for d in (1, 3, 2):
+        feat_copies[4 + d].wait_recv()
+
+    for k in (3, 2, 1, 0):
+
+        @pl.loop(0, SEND // 256)
+        def _(h):
+            cols = pl.ds(pl.multiple_of(h * 256, 256), 256)
+            fsend[k, :, cols] = nn(feat[...], pick[k, :, cols]).astype(BF16)
+
+        dom_copies[FWD, k] = dom_start(FWD, k, fsend.at[k], frecv.at[k], to_dom(k))
+        if k == 3:
+            hfs[...] = nt(hub_pick[...], feat[...]).astype(BF16)
+            for i in range(4):
+                dom_copies[HUBF, i] = dom_start(HUBF, i, hfs, hfr.at[i], to_dom(i))
+
+    for k in (2, 1, 0):
+        send_back(k)
+
     @pl.loop(0, HUBS // 256)
     def _(h):
         col = pl.multiple_of(HUB0 + h * 256, 256)
@@ -351,28 +391,6 @@
     for k in range(4):
         rows = pl.ds(pl.multiple_of(from_dom(k) * HUB_DEV, HUB_DEV), HUB_DEV)
         dom_copies[HUBB, k] = dom_start(HUBB, k, hbs.at[rows], hbr.at[k], from_dom(k))
-
-    for d in (1, 3, 2):
-        feat_copies[d].wait_recv()
-        owner = 2 * lax.rem(y - d + 4, 4) + core
-        c = tile_copy(FEAT, 4 + d, feat.at[rows32(owner)], feat.at[rows32(owner)], partner)
-        c.start()
-        feat_copies[4 + d] = c
-    feat_copies[0].wait_recv()
-    for d in (1, 3, 2):
-        feat_copies[4 + d].wait_recv()
-
-    hfs[...] = nt(hub_pick[...], feat[...]).astype(BF16)
-    for k in range(4):
-        dom_copies[HUBF, k] = dom_start(HUBF, k, hfs, hfr.at[k], to_dom(k))
-    for k in (3, 2, 1, 0):
-
-        @pl.loop(0, SEND // 256)
-        def _(h):
-            cols = pl.ds(pl.multiple_of(h * 256, 256), 256)
-            fsend[k, :, cols] = nn(feat[...], pick[k, :, cols]).astype(BF16)
-
-        dom_copies[FWD, k] = dom_start(FWD, k, fsend.at[k], frecv.at[k], to_dom(k))
 
     own = pl.ds(pl.multiple_of(j * OWN, OWN), OWN)
 
@@ -386,8 +404,13 @@
     grads[:, own] = nn(dagg[...], adj[:, 0:OWN])
     wgrad[0:32, :] = nn(feat_ref[...], cot_ref[...])
     wgrad[64:72, :] = nn(jnp.ones((8, ROWS), BF16), cot_ref[...])
-
-    for k in (3, 2, 1, 0):
+    for c in weight_copies[NT - 1 :]:
+        c.wait_recv()
+    ws_t = ws[...].astype(F32).T.astype(BF16)
+    mixed[...] = nn(ws_t, feat[:, own])
+    wn_t[...] = wn[...].astype(F32).T.astype(BF16)
+
+    def take_back(k):
         dom_copies[BWD, k].wait_recv()
 
         @pl.loop(0, ROWS // 256)
@@ -395,25 +418,7 @@
             rows = pl.ds(pl.multiple_of(r * 256, 256), 256)
             grads[:, rows] = grads[:, rows] + nt(brecv[k], pick[k, rows, :])
 
-    for k in range(4):
-        dom_copies[HUBB, k].wait_recv()
-    hub_back = jnp.concatenate([hbr[k].astype(F32) for k in range(4)], axis=0)
-    hub_back = jnp.concatenate([hub_back, jnp.zeros_like(hub_back)], axis=0).T.astype(BF16)
-
-    @pl.loop(0, ROWS // 256)
-    def _(r):
-        rows = pl.ds(pl.multiple_of(r * 256, 256), 256)
-        table = jnp.concatenate([hub_pick[:, rows]] * 8, axis=0)
-        grads[:, rows] = grads[:, rows] + nn(hub_back, table)
-        grad_send[:, rows] = grads[:, rows].astype(BF16)
-
-    grad_copies = []
-    for d in range(1, NT):
-        c = tile_copy(
-            GRAD, d, grad_send.at[rows32(lax.rem(j + d, NT))], grad_recv.at[d], peer(d)
-        )
-        c.start()
-        grad_copies.append(c)
+    take_back(3)
 
     for k in range(4):
         dom_copies[HUBF, k].wait_recv()
@@ -438,34 +443,44 @@
                 frecv[k], adj[rows, EDGE0 + k * SEND : EDGE0 + (k + 1) * SEND]
             )
 
-    @pl.loop(0, NT)
+    def block(index):
+        return pl.ds(pl.multiple_of(index * OWN, OWN), OWN)
+
+    def y_at(d):
+        return lax.rem(y + d, 4)
+
+    first = []
+    for d in (2, 1, 3, 0):
+        c = tile_copy(
+            ACC, 4 + d, acc.at[:, block(2 * y_at(d) + 1 - core)], acc_pair.at[d], partner
+        )
+        c.start()
+        first.append(c)
+    acc_copies = []
+    for i, d in enumerate((2, 1, 3)):
+        first[i].wait_recv()
+        acc_send[d] = (acc[:, block(2 * y_at(d) + core)] + acc_pair[d]).astype(BF16)
+        c = tile_copy(ACC, d, acc_send.at[d], acc_recv.at[d], at_y(d))
+        c.start()
+        acc_copies.append(c)
+    first[3].wait_recv()
+    acc_pair[0] = acc[:, own] + acc_pair[0]
+
+    for k in range(4):
+        dom_copies[HUBB, k].wait_recv()
+    hub_back = jnp.concatenate([hbr[k].astype(F32) for k in range(4)], axis=0)
+    hub_back = jnp.concatenate([hub_back, jnp.zeros_like(hub_back)], axis=0).T.astype(BF16)
+
+    @pl.loop(0, ROWS // 256)
     def _(r):
         rows = pl.ds(pl.multiple_of(r * 256, 256), 256)
-        acc_send[r] = acc[:, rows].astype(BF16)
-
-    acc_copies = []
-    for d in range(1, NT):
-        c = tile_copy(ACC, d, acc_send.at[lax.rem(j + d, NT)], acc_recv.at[d], peer(d))
-        c.start()
-        acc_copies.append(c)
-
-    for c in grad_copies:
-        c.wait_recv()
-    total = grads[rows32(j), :]
-    for d in range(1, NT):
-        total = total + grad_recv[d].astype(F32)
-    grad_out[...] = grad_out[...] + total
-
-    for c in weight_copies[NT - 1 :]:
-        c.wait_recv()
-    ws_t = ws[...].astype(F32).T.astype(BF16)
-    wn_t = wn[...].astype(F32).T.astype(BF16)
-    bias_t = jnp.broadcast_to(bias_ref[...], (BLK, CH)).T
-    mixed = nn(ws_t, feat[:, own])
+        table = jnp.concatenate([hub_pick[:, rows]] * 8, axis=0)
+        grads[:, rows] = grads[:, rows] + nn(hub_back, table)
+
     for c in acc_copies:
         c.wait_recv()
-    total = acc[:, own]
-    for d in range(1, NT):
+    total = acc_pair[0]
+    for d in range(1, 4):
         total = total + acc_recv[d].astype(F32)
     for h in range(2):
         cols = slice(h * BLK, (h + 1) * BLK)
@@ -479,10 +494,12 @@
         c.start()
         agg_copies.append(c)
     agg_recv[:, own] = agg_send[rows32(j), :]
-    mixed = mixed + nn(wn_t, agg_send[...])
+    bias_t = jnp.broadcast_to(bias_ref[...], (BLK, CH)).T
     for h in range(2):
         cols = slice(h * BLK, (h + 1) * BLK)
-        hid_send[:, cols] = (mixed[:, cols] + bias_t).astype(BF16)
+        hid_send[:, cols] = (
+            mixed[:, cols] + nn(wn_t[...], agg_send[:, cols]) + bias_t
+        ).astype(BF16)
     hid_copies = []
     for d in range(1, NT):
         c = tile_copy(
@@ -517,6 +534,9 @@
         c.start()
         x_copies.append(c)
     xrecv[x] = xsend[0]
+
+    take_back(2)
+
     for c in x_copies:
         c.wait_recv()
     total = xrecv[0]
@@ -536,6 +556,9 @@
         c.start()
         z_copies.append(c)
     zrecv[z] = zsend[...]
+
+    take_back(1)
+
     for c in z_copies:
         c.wait_recv()
     total = zrecv[0]
@@ -559,6 +582,26 @@
     gself_out[chunk(x), :] = gsend[0:8, :]
     gneigh_out[chunk(x), :] = gsend[8:16, :]
 
+    take_back(0)
+
+    first = []
+    for d in (2, 1, 3, 0):
+        grad_pair_send[d] = grads[rows32(2 * y_at(d) + 1 - core), :].astype(BF16)
+        c = tile_copy(GRAD, 4 + d, grad_pair_send.at[d], grad_pair.at[d], partner)
+        c.start()
+        first.append(c)
+    grad_copies = []
+    for i, d in enumerate((2, 1, 3)):
+        first[i].wait_recv()
+        grad_send[d] = (
+            grads[rows32(2 * y_at(d) + core), :] + grad_pair[d].astype(F32)
+        ).astype(BF16)
+        c = tile_copy(GRAD, d, grad_send.at[d], grad_recv.at[d], at_y(d))
+        c.start()
+        grad_copies.append(c)
+    first[3].wait_recv()
+    grad_out[...] = grad_out[...] + grads[rows32(j), :] + grad_pair[0].astype(F32)
+
     for c in hid_copies:
         c.wait_recv()
     hid_out[...] = hid_recv[...]
@@ -569,10 +612,20 @@
         gself_out[chunk(origin), :] = grecv[d, 0:8, :]
         gneigh_out[chunk(origin), :] = grecv[d, 8:16, :]
 
-    groups = (deg_copies, weight_copies, list(feat_copies.values()), grad_copies, acc_copies)
-    for group in groups + (agg_copies, hid_copies, x_copies, z_copies, g_copies):
-        for c in group:
-            c.wait_send()
+    for c in grad_copies:
+        c.wait_recv()
+    total = grad_out[...]
+    for d in range(1, 4):
+        total = total + grad_recv[d].astype(F32)
+    grad_out[...] = total
+
+    for c in deg_copies + weight_copies + list(feat_copies.values()) + agg_copies + hid_copies:
+        c.wait_send()
+    for c in x_copies + z_copies + g_copies + acc_copies + grad_copies:
+        c.wait_send()
+    for d in range(4):
+        tile_copy(ACC, 4 + d, acc.at[:, block(0)], acc_pair.at[d], partner).wait_send()
+        tile_copy(GRAD, 4 + d, grad_pair_send.at[d], grad_pair.at[d], partner).wait_send()
     for (cat, k), c in dom_copies.items():
         if k == 0:
 
@@ -581,6 +634,22 @@
                 c.wait_send()
         else:
             c.wait_send()
+
+
+def finish_kernel(hid, grad, gself, gneigh, gbias, hid_o, grad_o, gself_o, gneigh_o, gbias_o):
+    hid_o[...] = hid[...]
+    grad_o[...] = grad[...]
+    gself_o[...] = gself[...]
+    gneigh_o[...] = gneigh[...]
+    gbias_o[...] = gbias[...]
+
+
+def finish(*parts):
+    return pl.pallas_call(
+        finish_kernel,
+        out_shape=tuple(jax.ShapeDtypeStruct(p.shape, p.dtype) for p in parts),
+        name="finish",
+    )(*parts)
 
 
 def run_layer(feat_t, w_self, w_neigh, bias, cot, hubs, sends, counts, adjacency, degree):
@@ -619,10 +688,15 @@
             pltpu.VMEM((CH, ROWS), BF16),
             pltpu.VMEM((CH, ROWS), F32),
             pltpu.VMEM((CH, ROWS), F32),
-            pltpu.VMEM((NT, CH, OWN), BF16),
-            pltpu.VMEM((NT, CH, OWN), BF16),
-            pltpu.VMEM((CH, ROWS), BF16),
-            pltpu.VMEM((NT, 32, ROWS), BF16),
+            pltpu.VMEM((4, CH, OWN), F32),
+            pltpu.VMEM((4, CH, OWN), BF16),
+            pltpu.VMEM((4, CH, OWN), BF16),
+            pltpu.VMEM((4, 32, ROWS), BF16),
+            pltpu.VMEM((4, 32, ROWS), BF16),
+            pltpu.VMEM((4, 32, ROWS), BF16),
+            pltpu.VMEM((4, 32, ROWS), BF16),
+            pltpu.VMEM((CH, OWN), F32),
+            pltpu.VMEM((CH, CH), BF16),
             pltpu.VMEM((CH, OWN), BF16),
             pltpu.VMEM((32, ROWS), BF16),
             pltpu.VMEM((CH, OWN), BF16),
@@ -694,7 +768,7 @@
     codes = jnp.where(live & mine, dst * 64 + slot * 2 + counted, -1).astype(jnp.int32)
 
     adjacency, degree = build_adjacency(codes, tile_mask[0])
-    hidden_t, grad_t, grad_self, grad_neigh, grad_bias = run_layer(
+    parts = run_layer(
         features.T,
         w_self,
         w_neigh,
@@ -706,6 +780,7 @@
         adjacency,
         degree,
     )
+    hidden_t, grad_t, grad_self, grad_neigh, grad_bias = finish(*parts)
     return (hidden_t.T, grad_t.T, grad_self, grad_neigh, grad_bias[0])
 
 

time: 134 us -> 124 us (0.925)
  local copies, waits for them, and re-layouts: 11.5 us -> 0 us
    unnamed x9 -> x0, local copies, waits for them, and re-layouts: 11.5 us -> none
    pallas_call x0 -> x1, Pallas kernels: none -> 1.78 us  [finish(): pl.pallas_call(finish_kernel, out_shape=tuple((jax.ShapeDtypeStruct(p.sha...]
where the time goes in v2:
time: 124 us
  Pallas kernels  120 us (97%)
  other arithmetic  2.01 us (2%)
  between operations  1.32 us (1%)
    pallas_call x1, Pallas kernels, run_layer(): pl.pallas_call(layer_kernel, out_shape=(jax.ShapeDtypeStruct((32, ROWS),...  109 us
    pallas_call x1, Pallas kernels, build_adjacency(): pl.pallas_call(build_kernel, out_shape=(jax.ShapeDtypeStruct((ROWS, COLS)...  9.2 us

profile of v2, /device:TPU:1, one launch (start us, length us, event | category | flops | bytes accessed | tf_op | source)
XLA Modules:
  0.0 123.5 jit_solution(15636990825055707517)
XLA Ops:
  1.3 0.7 multiply_reduce_fusion
  2.0 0.7 reduce
  2.7 0.6 fusion.11.code_ref
  3.3 9.2 %adjacency.1 = (bf16[2048,2816]{1,0:T(8,128)(2,1)}, f32[16,128]{1,0:T(8,128)}) custom-call(s32[296]{0:T(512)} %fusion.11.code_ref, bf16[296,128,128]{2,1,0:T(8,128)(2,1)} %bitcast.8), custom_call_target="tpu_custom_call" | custom-call | tf_op jit(solution)/shard_map/adjacency/pallas_call | solution.py:93
  12.5 109.2 %layer.1 = (bf16[32,2048]{1,0:T(8,128)(2,1)}, f32[32,2048]{1,0:T(8,128)}, f32[32,256]{1,0:T(8,128)}, f32[32,256]{1,0:T(8,128)}, f32[1,256]{1,0:T(1,128)}) custom-call(bf16[32,2048]{1,0:T(8,128)(2,1)} %bitcast.9, bf16[32,256]{1,0:T(8,128)(2,1)} %ws_ref.1, bf16[32,256]{1,0:T(8,128)(2,1)} %wn_ref.1, f32[1,256]{1,0:T(1,128)} %bitcast.10, ...), custom_call_target="tpu_custom_call" | custom-call | tf_op jit(solution)/shard_map/layer/pallas_call | solution.py:659
  121.7 1.8 %finish.1 = (bf16[32,2048]{1,0:T(8,128)(2,1)}, f32[32,2048]{1,0:T(8,128)}, f32[32,256]{1,0:T(8,128)}, f32[32,256]{1,0:T(8,128)}, f32[1,256]{1,0:T(1,128)}) custom-call(bf16[32,2048]{1,0:T(8,128)(2,1)} %get-tuple-element.19.hid, f32[32,2048]{1,0:T(8,128)} %get-tuple-element.20.grad, f32[32,256]{1,0:T(8,128)} %get-tuple-element.21.gself, ...), custom_call_target="tpu_custom_call" | custom-call | tf_op jit(solution)/shard_map/finish/pallas_call | solution.py:648

commit v3 on v2

--- a/solution.py
+++ b/solution.py
@@ -40,14 +40,44 @@
     return lax.dot_general(a, b, (((1,), (1,)), ((), ())), preferred_element_type=F32)
 
 
-def build_kernel(code_ref, mask_ref, a_ref, deg_ref, listed, ring, row_total, sems):
+def first_step(j):
+    return lax.rem(j // 2 + lax.rem(j, 2) + 2, NX)
+
+
+def build_kernel(
+    src_ref, dst_ref, live_ref, mask_ref, a_ref, deg_ref, listed, ring, row_total, sems
+):
     cap = mask_ref.shape[0]
-
-    def scan(t, n):
-        listed[n] = t
-        return n + (code_ref[t] >= 0).astype(jnp.int32)
-
-    count = lax.fori_loop(0, cap, scan, jnp.int32(0))
+    me = lax.axis_index("dom")
+    j = lax.axis_index("tile")
+    z, x = me // NX, lax.rem(me, NX)
+    own_blocks, hub_end = ROWS // BLK, (ROWS + HUBS) // BLK
+    live = live_ref[0]
+
+    def place(t):
+        src = src_ref[0, t]
+        edge = src - hub_end
+        sender = edge >> 2
+        k = (x - sender) & 3
+        owner = (z - (sender >> 2) + 2 * k) & 7
+        is_own, is_edge = src < own_blocks, src >= hub_end
+        mine = jnp.where(is_own, src >> 1, jnp.where(is_edge, owner, j)) == j
+        step = (k - first_step(j)) & 3
+        col = jnp.where(
+            is_own,
+            src & 1,
+            jnp.where(is_edge, EDGE0 // BLK + step * 4 + (edge & 3), src - own_blocks + 2),
+        )
+        return mine, col
+
+    def scan(group, n):
+        for i in range(8):
+            t = group * 8 + i
+            listed[n] = t
+            n = n + (place(t)[0] & (t < live)).astype(jnp.int32)
+        return n
+
+    count = lax.fori_loop(0, cap // 8, scan, jnp.int32(0))
 
     def fetch(i):
         slot = lax.rem(i, RING)
@@ -66,12 +96,15 @@
     @pl.loop(0, count)
     def _(i):
         fetch(i).wait()
-        code = code_ref[listed[i]]
+        t = listed[i]
+        col_block = place(t)[1]
         tile = ring[lax.rem(i, RING)]
-        dst = pl.ds(pl.multiple_of((code // 64) * BLK, BLK), BLK)
-        col = pl.ds(pl.multiple_of((lax.rem(code, 64) // 2) * BLK, BLK), BLK)
+        dst = pl.ds(pl.multiple_of(dst_ref[0, t] * BLK, BLK), BLK)
+        col = pl.ds(pl.multiple_of(col_block * BLK, BLK), BLK)
         a_ref[dst, col] = a_ref[dst, col] + tile
-        row_total[dst, :] = row_total[dst, :] + tile.astype(F32) * lax.rem(code, 2).astype(F32)
+        is_hub = (src_ref[0, t] >= own_blocks) & (src_ref[0, t] < hub_end)
+        counted = jnp.where(is_hub & (j != 0), 0.0, 1.0)
+        row_total[dst, :] = row_total[dst, :] + tile.astype(F32) * counted
 
         @pl.when(i + RING < count)
         def _():
@@ -89,17 +122,15 @@
         deg_ref[d : d + 1, :] = sums[0:1, :]
 
 
-def build_adjacency(codes, masks):
+def build_adjacency(src, dst, live, masks):
     return pl.pallas_call(
         build_kernel,
         out_shape=(
             jax.ShapeDtypeStruct((ROWS, COLS), BF16),
             jax.ShapeDtypeStruct((ROWS // BLK, BLK), F32),
         ),
-        in_specs=[
-            pl.BlockSpec(memory_space=pltpu.SMEM),
-            pl.BlockSpec(memory_space=pl.ANY),
-        ],
+        in_specs=[pl.BlockSpec(memory_space=pltpu.SMEM)] * 3
+        + [pl.BlockSpec(memory_space=pl.ANY)],
         out_specs=(
             pl.BlockSpec(memory_space=pltpu.VMEM),
             pl.BlockSpec(memory_space=pltpu.VMEM),
@@ -112,7 +143,7 @@
         ],
         compiler_params=pltpu.CompilerParams(vmem_limit_bytes=60 * 2**20),
         name="adjacency",
-    )(codes, masks)
+    )(src, dst, live, masks)
 
 
 def layer_kernel(
@@ -161,6 +192,8 @@
     wn_t,
     agg_send,
     agg_recv,
+    agg_rows,
+    share,
     hid_send,
     hid_recv,
     wgrad,
@@ -200,11 +233,18 @@
     def at_z(d):
         return (lax.rem(z + d, NZ) * NX + x, j)
 
-    def to_dom(k):
-        return lax.rem(z + j - 2 * k + 2 * NZ, NZ) * NX + lax.rem(x + k, NX)
-
-    def from_dom(k):
-        return lax.rem(z - j + 2 * k + 2 * NZ, NZ) * NX + lax.rem(x - k + NX, NX)
+    start = first_step(j)
+
+    def dom_at(dz, dx):
+        return lax.rem(z + dz + 2 * NZ, NZ) * NX + lax.rem(x + dx + 2 * NX, NX)
+
+    def to_dom(i):
+        k = lax.rem(start + i, NX)
+        return dom_at(j - 2 * k, k)
+
+    def from_dom(i):
+        k = lax.rem(start + i, NX)
+        return dom_at(2 * k - j, -k)
 
     barrier = pltpu.get_barrier_semaphore()
 
@@ -217,14 +257,14 @@
         greet(at_x(d))
     for d in range(1, NZ):
         greet(at_z(d))
-    for k in range(1, 4):
+    for k in (0, 1, 3):
         greet((to_dom(k), j))
         greet((from_dom(k), j))
 
     @pl.when(j != 0)
     def _():
-        greet((to_dom(0), j))
-        greet((from_dom(0), j))
+        greet((to_dom(2), j))
+        greet((from_dom(2), j))
 
     pl.semaphore_wait(barrier, 23 + 2 * (j != 0).astype(jnp.int32))
 
@@ -246,6 +286,15 @@
     def rows32(index):
         return pl.ds(pl.multiple_of(index * 32, 32), 32)
 
+    deg_copies, weight_copies = [], []
+    for d in range(1, NT):
+        c = tile_copy(DEG, d, deg_ref, degs.at[d], peer(d))
+        c.start()
+        deg_copies.append(c)
+    for d in range(1, NT):
+        c = tile_copy(WN, d, wn_ref, wn.at[rows32(j)], peer(d))
+        c.start()
+        weight_copies.append(c)
     feat_copies = {}
     for d in (1, 3, 2):
         c = tile_copy(FEAT, d, feat_ref, feat.at[rows32(j)], at_y(d))
@@ -254,15 +303,6 @@
     c = tile_copy(FEAT, 0, feat_ref, feat.at[rows32(j)], partner)
     c.start()
     feat_copies[0] = c
-    deg_copies, weight_copies = [], []
-    for d in range(1, NT):
-        c = tile_copy(DEG, d, deg_ref, degs.at[d], peer(d))
-        c.start()
-        deg_copies.append(c)
-    for d in range(1, NT):
-        c = tile_copy(WN, d, wn_ref, wn.at[rows32(j)], peer(d))
-        c.start()
-        weight_copies.append(c)
     for d in range(1, NT):
         c = tile_copy(WS, d, ws_ref, ws.at[rows32(j)], peer(d))
         c.start()
@@ -273,7 +313,8 @@
     ws[rows32(j), :] = ws_ref[...]
 
     lanes = lax.broadcasted_iota(jnp.int32, (1, SEND), 1)
-    for k in range(4):
+
+    def make_pick(k):
         q = to_dom(k)
         index = jnp.where(lanes < count_ref[0, q], send_ref[0, pl.ds(q, 1), :], -1)
 
@@ -283,6 +324,8 @@
             row = lax.broadcasted_iota(jnp.int32, (128, SEND), 0) + base
             pick[k, pl.ds(base, 128), :] = (row == index).astype(F32).astype(BF16)
 
+    for k in (0, 1):
+        make_pick(k)
     slot = lax.broadcasted_iota(jnp.int32, (HUB_DEV, BLK), 0)
     hub_index = jnp.zeros((HUB_DEV, BLK), jnp.int32)
     for i in range(HUB_DEV):
@@ -297,9 +340,6 @@
         c = tile_copy(FEAT, 4 + d, feat.at[rows32(owner)], feat.at[rows32(owner)], partner)
         c.start()
         feat_copies[4 + d] = c
-
-    relay(1)
-    relay(3)
 
     for c in deg_copies:
         c.wait_recv()
@@ -320,7 +360,8 @@
                 part[:, h * BLK : (h + 1) * BLK] / floor
             ).astype(BF16)
 
-    relay(2)
+    relay(1)
+    relay(3)
     load_adj.wait()
 
     def dom_copy(cat, k, src, dst, device):
@@ -335,7 +376,7 @@
 
     def dom_start(cat, k, src, dst, device):
         copy = dom_copy(cat, k, src, dst, device)
-        if k == 0:
+        if k == 2:
 
             @pl.when(j != 0)
             def _():
@@ -346,11 +387,20 @@
                 pltpu.make_async_copy(src, dst, jrs.at[cat, k]).start()
         else:
             copy.start()
-        return copy
-
-    dom_copies = {}
-
-    def send_back(k):
+
+    def dom_wait(cat, k, dst):
+        dom_copy(cat, k, dst, dst, me).wait_recv()
+
+    def dom_sent(cat, k, src):
+        if k == 2:
+
+            @pl.when(j != 0)
+            def _():
+                dom_copy(cat, k, src, src, me).wait_send()
+        else:
+            dom_copy(cat, k, src, src, me).wait_send()
+
+    def make_back(k):
         @pl.loop(0, SEND // 256)
         def _(h):
             col = pl.multiple_of(EDGE0 + k * SEND + h * 256, 256)
@@ -358,29 +408,36 @@
                 dagg[...], adj[:, pl.ds(col, 256)]
             ).astype(BF16)
 
-        dom_copies[BWD, k] = dom_start(BWD, k, bsend.at[k], brecv.at[k], from_dom(k))
-
-    send_back(3)
+    def send_back(k):
+        dom_start(BWD, k, bsend.at[k], brecv.at[k], from_dom(k))
+
+    make_back(1)
+    send_back(1)
+    make_back(2)
+    send_back(2)
+    relay(2)
+    for k in (2, 3):
+        make_pick(k)
 
     feat_copies[0].wait_recv()
     for d in (1, 3, 2):
         feat_copies[4 + d].wait_recv()
 
-    for k in (3, 2, 1, 0):
+    for k in range(4):
 
         @pl.loop(0, SEND // 256)
         def _(h):
             cols = pl.ds(pl.multiple_of(h * 256, 256), 256)
             fsend[k, :, cols] = nn(feat[...], pick[k, :, cols]).astype(BF16)
 
-        dom_copies[FWD, k] = dom_start(FWD, k, fsend.at[k], frecv.at[k], to_dom(k))
-        if k == 3:
+        dom_start(FWD, k, fsend.at[k], frecv.at[k], to_dom(k))
+        if k == 1:
             hfs[...] = nt(hub_pick[...], feat[...]).astype(BF16)
             for i in range(4):
-                dom_copies[HUBF, i] = dom_start(HUBF, i, hfs, hfr.at[i], to_dom(i))
-
-    for k in (2, 1, 0):
-        send_back(k)
+                dom_start(HUBF, i, hfs, hfr.at[i], to_dom(i))
+
+    for k in (0, 3):
+        make_back(k)
 
     @pl.loop(0, HUBS // 256)
     def _(h):
@@ -390,7 +447,7 @@
 
     for k in range(4):
         rows = pl.ds(pl.multiple_of(from_dom(k) * HUB_DEV, HUB_DEV), HUB_DEV)
-        dom_copies[HUBB, k] = dom_start(HUBB, k, hbs.at[rows], hbr.at[k], from_dom(k))
+        dom_start(HUBB, k, hbs.at[rows], hbr.at[k], from_dom(k))
 
     own = pl.ds(pl.multiple_of(j * OWN, OWN), OWN)
 
@@ -411,17 +468,17 @@
     wn_t[...] = wn[...].astype(F32).T.astype(BF16)
 
     def take_back(k):
-        dom_copies[BWD, k].wait_recv()
+        dom_wait(BWD, k, brecv.at[k])
 
         @pl.loop(0, ROWS // 256)
         def _(r):
             rows = pl.ds(pl.multiple_of(r * 256, 256), 256)
             grads[:, rows] = grads[:, rows] + nt(brecv[k], pick[k, rows, :])
 
-    take_back(3)
+    take_back(1)
 
     for k in range(4):
-        dom_copies[HUBF, k].wait_recv()
+        dom_wait(HUBF, k, hfr.at[k])
     hub_src[...] = jnp.zeros((HUBS, CH), BF16)
     for k in range(4):
         rows = pl.ds(pl.multiple_of(from_dom(k) * HUB_DEV, HUB_DEV), HUB_DEV)
@@ -433,15 +490,22 @@
         rows = pl.ds(pl.multiple_of(r * 256, 256), 256)
         acc[:, rows] = acc[:, rows] + nt(hub_src_t, adj[rows, HUB0:EDGE0])
 
-    for k in (3, 2, 1, 0):
-        dom_copies[FWD, k].wait_recv()
+    def take_rows(k, rows):
+        acc[:, rows] = acc[:, rows] + nt(
+            frecv[k], adj[rows, EDGE0 + k * SEND : EDGE0 + (k + 1) * SEND]
+        )
+
+    for k in range(4):
+        dom_sent(FWD, k, fsend.at[k])
+    for k in (0, 3):
+        send_back(k)
+
+    for k in (2, 1, 0):
+        dom_wait(FWD, k, frecv.at[k])
 
         @pl.loop(0, ROWS // 256)
         def _(r):
-            rows = pl.ds(pl.multiple_of(r * 256, 256), 256)
-            acc[:, rows] = acc[:, rows] + nt(
-                frecv[k], adj[rows, EDGE0 + k * SEND : EDGE0 + (k + 1) * SEND]
-            )
+            take_rows(k, pl.ds(pl.multiple_of(r * 256, 256), 256))
 
     def block(index):
         return pl.ds(pl.multiple_of(index * OWN, OWN), OWN)
@@ -449,13 +513,16 @@
     def y_at(d):
         return lax.rem(y + d, 4)
 
+    dom_wait(FWD, 3, frecv.at[3])
     first = []
     for d in (2, 1, 3, 0):
-        c = tile_copy(
-            ACC, 4 + d, acc.at[:, block(2 * y_at(d) + 1 - core)], acc_pair.at[d], partner
-        )
+        rows = block(2 * y_at(d) + 1 - core)
+        take_rows(3, rows)
+        c = tile_copy(ACC, 4 + d, acc.at[:, rows], acc_pair.at[d], partner)
         c.start()
         first.append(c)
+    for d in (2, 1, 3, 0):
+        take_rows(3, block(2 * y_at(d) + core))
     acc_copies = []
     for i, d in enumerate((2, 1, 3)):
         first[i].wait_recv()
@@ -466,8 +533,18 @@
     first[3].wait_recv()
     acc_pair[0] = acc[:, own] + acc_pair[0]
 
+    for r in range(ROWS // BLK):
+        cols = slice(r * BLK, (r + 1) * BLK)
+        share[:, cols] = (acc[:, cols] / degs[0, r : r + 1, :]).astype(BF16)
+    agg_send[...] = nn(share[...], cot_ref[...])
+    agg_copies = []
+    for d in range(1, NT):
+        c = tile_copy(AGG, d, agg_send.at[rows32(lax.rem(j + d, NT))], agg_recv.at[d], peer(d))
+        c.start()
+        agg_copies.append(c)
+
     for k in range(4):
-        dom_copies[HUBB, k].wait_recv()
+        dom_wait(HUBB, k, hbr.at[k])
     hub_back = jnp.concatenate([hbr[k].astype(F32) for k in range(4)], axis=0)
     hub_back = jnp.concatenate([hub_back, jnp.zeros_like(hub_back)], axis=0).T.astype(BF16)
 
@@ -477,41 +554,12 @@
         table = jnp.concatenate([hub_pick[:, rows]] * 8, axis=0)
         grads[:, rows] = grads[:, rows] + nn(hub_back, table)
 
-    for c in acc_copies:
-        c.wait_recv()
-    total = acc_pair[0]
-    for d in range(1, 4):
-        total = total + acc_recv[d].astype(F32)
-    for h in range(2):
-        cols = slice(h * BLK, (h + 1) * BLK)
-        floor = degs[0, pl.ds(2 * j + h, 1), :]
-        agg_send[:, cols] = (total[:, cols] / floor).astype(BF16)
-    agg_copies = []
-    for d in range(1, NT):
-        c = tile_copy(
-            AGG, d, agg_send.at[rows32(lax.rem(j + d, NT))], agg_recv.at[:, own], peer(d)
-        )
-        c.start()
-        agg_copies.append(c)
-    agg_recv[:, own] = agg_send[rows32(j), :]
-    bias_t = jnp.broadcast_to(bias_ref[...], (BLK, CH)).T
-    for h in range(2):
-        cols = slice(h * BLK, (h + 1) * BLK)
-        hid_send[:, cols] = (
-            mixed[:, cols] + nn(wn_t[...], agg_send[:, cols]) + bias_t
-        ).astype(BF16)
-    hid_copies = []
-    for d in range(1, NT):
-        c = tile_copy(
-            HID, d, hid_send.at[rows32(lax.rem(j + d, NT))], hid_recv.at[:, own], peer(d)
-        )
-        c.start()
-        hid_copies.append(c)
-    hid_recv[:, own] = hid_send[rows32(j), :]
-
     for c in agg_copies:
         c.wait_recv()
-    wgrad[32:64, :] = nn(agg_recv[...], cot_ref[...])
+    total = agg_send[rows32(j), :]
+    for d in range(1, NT):
+        total = total + agg_recv[d]
+    wgrad[32:64, :] = total
 
     def chunk(index):
         return pl.ds(pl.multiple_of(index * 8, 8), 8)
@@ -535,7 +583,31 @@
         x_copies.append(c)
     xrecv[x] = xsend[0]
 
-    take_back(2)
+    for c in acc_copies:
+        c.wait_recv()
+    total = acc_pair[0]
+    for d in range(1, 4):
+        total = total + acc_recv[d].astype(F32)
+    for h in range(2):
+        cols = slice(h * BLK, (h + 1) * BLK)
+        floor = degs[0, pl.ds(2 * j + h, 1), :]
+        agg_rows[:, cols] = (total[:, cols] / floor).astype(BF16)
+    bias_t = jnp.broadcast_to(bias_ref[...], (BLK, CH)).T
+    for h in range(2):
+        cols = slice(h * BLK, (h + 1) * BLK)
+        hid_send[:, cols] = (
+            mixed[:, cols] + nn(wn_t[...], agg_rows[:, cols]) + bias_t
+        ).astype(BF16)
+    hid_copies = []
+    for d in range(1, NT):
+        c = tile_copy(
+            HID, d, hid_send.at[rows32(lax.rem(j + d, NT))], hid_recv.at[:, own], peer(d)
+        )
+        c.start()
+        hid_copies.append(c)
+    hid_recv[:, own] = hid_send[rows32(j), :]
+
+    take_back(0)
 
     for c in x_copies:
         c.wait_recv()
@@ -557,7 +629,7 @@
         z_copies.append(c)
     zrecv[z] = zsend[...]
 
-    take_back(1)
+    take_back(2)
 
     for c in z_copies:
         c.wait_recv()
@@ -582,7 +654,7 @@
     gself_out[chunk(x), :] = gsend[0:8, :]
     gneigh_out[chunk(x), :] = gsend[8:16, :]
 
-    take_back(0)
+    take_back(3)
 
     first = []
     for d in (2, 1, 3, 0):
@@ -626,14 +698,10 @@
     for d in range(4):
         tile_copy(ACC, 4 + d, acc.at[:, block(0)], acc_pair.at[d], partner).wait_send()
         tile_copy(GRAD, 4 + d, grad_pair_send.at[d], grad_pair.at[d], partner).wait_send()
-    for (cat, k), c in dom_copies.items():
-        if k == 0:
-
-            @pl.when(j != 0)
-            def _():
-                c.wait_send()
-        else:
-            c.wait_send()
+    for k in range(4):
+        dom_sent(BWD, k, bsend.at[k])
+        dom_sent(HUBF, k, hfs)
+        dom_sent(HUBB, k, hbs.at[pl.ds(0, HUB_DEV)])
 
 
 def finish_kernel(hid, grad, gself, gneigh, gbias, hid_o, grad_o, gself_o, gneigh_o, gbias_o):
@@ -697,8 +765,10 @@
             pltpu.VMEM((4, 32, ROWS), BF16),
             pltpu.VMEM((CH, OWN), F32),
             pltpu.VMEM((CH, CH), BF16),
+            pltpu.VMEM((CH, CH), F32),
+            pltpu.VMEM((NT, 32, CH), F32),
             pltpu.VMEM((CH, OWN), BF16),
-            pltpu.VMEM((32, ROWS), BF16),
+            pltpu.VMEM((CH, ROWS), BF16),
             pltpu.VMEM((CH, OWN), BF16),
             pltpu.VMEM((32, ROWS), BF16),
             pltpu.VMEM((72, CH), F32),
@@ -741,33 +811,7 @@
     tile_count,
     tile_mask,
 ):
-    me = lax.axis_index("dom")
-    j = lax.axis_index("tile")
-    z, x = me // NX, me % NX
-
-    src, dst = tile_src[0], tile_dst[0]
-    live = jnp.arange(src.shape[0], dtype=jnp.int32) < tile_count[0]
-    own_blocks, hub_blocks = ROWS // BLK, HUBS // BLK
-    edge = src - own_blocks - hub_blocks
-    sender = edge // (SEND // BLK)
-    k = (x - sender) % NX
-    edge_owner = (z - sender // NX + 2 * k) % NZ
-    is_own = src < own_blocks
-    is_hub = jnp.logical_not(is_own) & (edge < 0)
-    mine = jnp.where(is_own, src // (OWN // BLK) == j, is_hub | (edge_owner == j))
-    slot = jnp.where(
-        is_own,
-        src % (OWN // BLK),
-        jnp.where(
-            is_hub,
-            src - own_blocks + HUB0 // BLK,
-            EDGE0 // BLK + k * (SEND // BLK) + edge % (SEND // BLK),
-        ),
-    )
-    counted = jnp.where(is_hub & (j != 0), 0, 1)
-    codes = jnp.where(live & mine, dst * 64 + slot * 2 + counted, -1).astype(jnp.int32)
-
-    adjacency, degree = build_adjacency(codes, tile_mask[0])
+    adjacency, degree = build_adjacency(tile_src, tile_dst, tile_count, tile_mask[0])
     parts = run_layer(
         features.T,
         w_self,

time: 124 us -> 115 us (0.927)
  Pallas kernels: 120 us -> 113 us
  other arithmetic: 2.01 us -> 0 us
    pallas_call x1, Pallas kernels: 109 us -> 102 us  [run_layer(): pl.pallas_call(layer_kernel, out_shape=(jax.ShapeDtypeStruct((32, ROWS),...]
where the time goes in v3:
time: 115 us
  Pallas kernels  113 us (98%)
  between operations  1.29 us (1%)
    pallas_call x1, Pallas kernels, run_layer(): pl.pallas_call(layer_kernel, out_shape=(jax.ShapeDtypeStruct((32, ROWS),...  102 us
    pallas_call x1, Pallas kernels, build_adjacency(): pl.pallas_call(build_kernel, out_shape=(jax.ShapeDtypeStruct((ROWS, COLS)...  9.36 us

profile of v3, /device:TPU:1, one launch (start us, length us, event | category | flops | bytes accessed | tf_op | source)
XLA Modules:
  0.0 114.6 jit_solution(13595866311449742980)
XLA Ops:
  1.3 9.4 %adjacency.1 = (bf16[2048,2816]{1,0:T(8,128)(2,1)}, f32[16,128]{1,0:T(8,128)}) custom-call(s32[1,296]{1,0:T(1,128)} %src_ref.1, s32[1,296]{1,0:T(1,128)} %dst_ref.1, s32[1]{0:T(128)S(6)} %copy.17.live_ref, bf16[296,128,128]{2,1,0:T(8,128)(2,1)} %bitcast.6), custom_call_target="tpu_custom_call" | custom-call | tf_op jit(solution)/shard_map/adjacency/pallas_call | solution.py:126
  10.7 102.2 %layer.1 = (bf16[32,2048]{1,0:T(8,128)(2,1)}, f32[32,2048]{1,0:T(8,128)}, f32[32,256]{1,0:T(8,128)}, f32[32,256]{1,0:T(8,128)}, f32[1,256]{1,0:T(1,128)}) custom-call(bf16[32,2048]{1,0:T(8,128)(2,1)} %bitcast.7, bf16[32,256]{1,0:T(8,128)(2,1)} %ws_ref.1, bf16[32,256]{1,0:T(8,128)(2,1)} %wn_ref.1, f32[1,256]{1,0:T(1,128)} %bitcast.8, ...), custom_call_target="tpu_custom_call" | custom-call | tf_op jit(solution)/shard_map/layer/pallas_call | solution.py:727
  112.9 1.8 %finish.1 = (bf16[32,2048]{1,0:T(8,128)(2,1)}, f32[32,2048]{1,0:T(8,128)}, f32[32,256]{1,0:T(8,128)}, f32[32,256]{1,0:T(8,128)}, f32[1,256]{1,0:T(1,128)}) custom-call(bf16[32,2048]{1,0:T(8,128)(2,1)} %get-tuple-element.19.hid, f32[32,2048]{1,0:T(8,128)} %get-tuple-element.20.grad, f32[32,256]{1,0:T(8,128)} %get-tuple-element.21.gself, ...), custom_call_target="tpu_custom_call" | custom-call | tf_op jit(solution)/shard_map/finish/pallas_call | solution.py:716

commit v4 on v3

--- a/solution.py
+++ b/solution.py
@@ -70,14 +70,24 @@
         )
         return mine, col
 
-    def scan(group, n):
-        for i in range(8):
-            t = group * 8 + i
-            listed[n] = t
-            n = n + (place(t)[0] & (t < live)).astype(jnp.int32)
+    def note(t, n):
+        listed[n] = t
+        return n + (place(t)[0] & (t < live)).astype(jnp.int32)
+
+    steps = ROWS // 64
+    per_step = cap // steps
+
+    def scan(r, n):
+        rows = pl.ds(pl.multiple_of(r * 64, 64), 64)
+        a_ref[rows, :] = jnp.zeros((64, COLS), BF16)
+        row_total[rows, :] = jnp.zeros((64, BLK), F32)
+        for i in range(per_step):
+            n = note(r * per_step + i, n)
         return n
 
-    count = lax.fori_loop(0, cap // 8, scan, jnp.int32(0))
+    count = lax.fori_loop(0, steps, scan, jnp.int32(0))
+    for t in range(steps * per_step, cap):
+        count = note(t, count)
 
     def fetch(i):
         slot = lax.rem(i, RING)
@@ -86,12 +96,6 @@
     @pl.loop(0, jnp.minimum(count, RING))
     def _(i):
         fetch(i).start()
-
-    @pl.loop(0, ROWS // 64)
-    def _(r):
-        start = pl.multiple_of(r * 64, 64)
-        a_ref[pl.ds(start, 64), :] = jnp.zeros((64, COLS), BF16)
-        row_total[pl.ds(start, 64), :] = jnp.zeros((64, BLK), F32)
 
     @pl.loop(0, count)
     def _(i):
@@ -110,16 +114,12 @@
         def _():
             fetch(i + RING).start()
 
-    ones = jnp.ones((8, BLK), F32)
+    ones = jnp.ones((8, BLK), BF16)
     for d in range(ROWS // BLK):
-        sums = lax.dot_general(
-            ones,
-            row_total[d * BLK : (d + 1) * BLK, :],
-            (((1,), (1,)), ((), ())),
-            precision=lax.Precision.HIGHEST,
-            preferred_element_type=F32,
-        )
-        deg_ref[d : d + 1, :] = sums[0:1, :]
+        part = row_total[d * BLK : (d + 1) * BLK, :]
+        high = part.astype(BF16)
+        low = (part - high.astype(F32)).astype(BF16)
+        deg_ref[d : d + 1, :] = (nt(ones, high) + nt(ones, low))[0:1, :]
 
 
 def build_adjacency(src, dst, live, masks):

time: 115 us -> 117 us (1.017)
  Pallas kernels: 113 us -> 115 us
    pallas_call x1, Pallas kernels: 102 us -> 104 us  [run_layer(): pl.pallas_call(layer_kernel, out_shape=(jax.ShapeDtypeStruct((32, ROWS),...]
where the time goes in v4:
time: 117 us; the launch traced here: 116 us
  Pallas kernels  115 us (98%)
  between operations  1.29 us (1%)
    pallas_call x1, Pallas kernels, run_layer(): pl.pallas_call(layer_kernel, out_shape=(jax.ShapeDtypeStruct((32, ROWS),...  104 us
    pallas_call x1, Pallas kernels, build_adjacency(): pl.pallas_call(build_kernel, out_shape=(jax.ShapeDtypeStruct((ROWS, COLS)...  9.61 us

profile of v4, /device:TPU:1, one launch (start us, length us, event | category | flops | bytes accessed | tf_op | source)
XLA Modules:
  0.0 116.3 jit_solution(13468651006124705890)
XLA Ops:
  1.3 9.6 %adjacency.1 = (bf16[2048,2816]{1,0:T(8,128)(2,1)}, f32[16,128]{1,0:T(8,128)}) custom-call(s32[1,296]{1,0:T(1,128)} %src_ref.1, s32[1,296]{1,0:T(1,128)} %dst_ref.1, s32[1]{0:T(128)S(6)} %copy.17.live_ref, bf16[296,128,128]{2,1,0:T(8,128)(2,1)} %bitcast.6), custom_call_target="tpu_custom_call" | custom-call | tf_op jit(solution)/shard_map/adjacency/pallas_call | solution.py:126
  10.9 103.6 %layer.1 = (bf16[32,2048]{1,0:T(8,128)(2,1)}, f32[32,2048]{1,0:T(8,128)}, f32[32,256]{1,0:T(8,128)}, f32[32,256]{1,0:T(8,128)}, f32[1,256]{1,0:T(1,128)}) custom-call(bf16[32,2048]{1,0:T(8,128)(2,1)} %bitcast.7, bf16[32,256]{1,0:T(8,128)(2,1)} %ws_ref.1, bf16[32,256]{1,0:T(8,128)(2,1)} %wn_ref.1, f32[1,256]{1,0:T(1,128)} %bitcast.8, ...), custom_call_target="tpu_custom_call" | custom-call | tf_op jit(solution)/shard_map/layer/pallas_call | solution.py:727
  114.5 1.8 %finish.1 = (bf16[32,2048]{1,0:T(8,128)(2,1)}, f32[32,2048]{1,0:T(8,128)}, f32[32,256]{1,0:T(8,128)}, f32[32,256]{1,0:T(8,128)}, f32[1,256]{1,0:T(1,128)}) custom-call(bf16[32,2048]{1,0:T(8,128)(2,1)} %get-tuple-element.19.hid, f32[32,2048]{1,0:T(8,128)} %get-tuple-element.20.grad, f32[32,256]{1,0:T(8,128)} %get-tuple-element.21.gself, ...), custom_call_target="tpu_custom_call" | custom-call | tf_op jit(solution)/shard_map/finish/pallas_call | solution.py:716

commit v5 on v4

--- a/solution.py
+++ b/solution.py
@@ -476,6 +476,7 @@
             grads[:, rows] = grads[:, rows] + nt(brecv[k], pick[k, rows, :])
 
     take_back(1)
+    take_back(2)
 
     for k in range(4):
         dom_wait(HUBF, k, hfr.at[k])
@@ -628,8 +629,6 @@
         c.start()
         z_copies.append(c)
     zrecv[z] = zsend[...]
-
-    take_back(2)
 
     for c in z_copies:
         c.wait_recv()

time: 117 us -> 114 us (0.974)
  Pallas kernels: 115 us -> 113 us
    pallas_call x1, Pallas kernels: 104 us -> 101 us  [run_layer(): pl.pallas_call(layer_kernel, out_shape=(jax.ShapeDtypeStruct((32, ROWS),...]
where the time goes in v5:
time: 114 us
  Pallas kernels  113 us (99%)
  between operations  1.29 us (1%)
    pallas_call x1, Pallas kernels, run_layer(): pl.pallas_call(layer_kernel, out_shape=(jax.ShapeDtypeStruct((32, ROWS),...  101 us
    pallas_call x1, Pallas kernels, build_adjacency(): pl.pallas_call(build_kernel, out_shape=(jax.ShapeDtypeStruct((ROWS, COLS)...  9.75 us

profile of v5, /device:TPU:1, one launch (start us, length us, event | category | flops | bytes accessed | tf_op | source)
XLA Modules:
  0.0 114.1 jit_solution(2495748951481208865)
XLA Ops:
  1.3 9.7 %adjacency.1 = (bf16[2048,2816]{1,0:T(8,128)(2,1)}, f32[16,128]{1,0:T(8,128)}) custom-call(s32[1,296]{1,0:T(1,128)} %src_ref.1, s32[1,296]{1,0:T(1,128)} %dst_ref.1, s32[1]{0:T(128)S(6)} %copy.17.live_ref, bf16[296,128,128]{2,1,0:T(8,128)(2,1)} %bitcast.6), custom_call_target="tpu_custom_call" | custom-call | tf_op jit(solution)/shard_map/adjacency/pallas_call | solution.py:126
  11.0 101.3 %layer.1 = (bf16[32,2048]{1,0:T(8,128)(2,1)}, f32[32,2048]{1,0:T(8,128)}, f32[32,256]{1,0:T(8,128)}, f32[32,256]{1,0:T(8,128)}, f32[1,256]{1,0:T(1,128)}) custom-call(bf16[32,2048]{1,0:T(8,128)(2,1)} %bitcast.7, bf16[32,256]{1,0:T(8,128)(2,1)} %ws_ref.1, bf16[32,256]{1,0:T(8,128)(2,1)} %wn_ref.1, f32[1,256]{1,0:T(1,128)} %bitcast.8, ...), custom_call_target="tpu_custom_call" | custom-call | tf_op jit(solution)/shard_map/layer/pallas_call | solution.py:726
  112.3 1.8 %finish.1 = (bf16[32,2048]{1,0:T(8,128)(2,1)}, f32[32,2048]{1,0:T(8,128)}, f32[32,256]{1,0:T(8,128)}, f32[32,256]{1,0:T(8,128)}, f32[1,256]{1,0:T(1,128)}) custom-call(bf16[32,2048]{1,0:T(8,128)(2,1)} %get-tuple-element.19.hid, f32[32,2048]{1,0:T(8,128)} %get-tuple-element.20.grad, f32[32,256]{1,0:T(8,128)} %get-tuple-element.21.gself, ...), custom_call_target="tpu_custom_call" | custom-call | tf_op jit(solution)/shard_map/finish/pallas_call | solution.py:715
